TPU v7x, 256 devices: a whole 4x4x8 slice. The times are simulated.
256 devices in a mesh: layer: 2 (over z_lo), row: 8 (over x, core), col: 16 (over y, z_hi).
Axes of the slice: x: 4, y: 4, z: 8 (z_hi: 4, z_lo: 2; z = z_hi * 2 + z_lo), core: 2. Of those that a mesh axis runs over, the one named last changes fastest.
Arguments:
- density: bfloat16 [512, 16, 2, 64, 64], P('row', 'col', 'layer'), as said below
- pattern: int32 [512, 16, 2], P('row', 'col', 'layer'), may hold values from -1 to 31, as said below
Outputs:
- squared: bfloat16 [512, 16, 2, 64, 64], P('row', 'col', 'layer')
- raised: bfloat16 [512, 16, 2, 64, 64], P('row', 'col', 'layer')
Inputs may be any that keep to these rules, and one draw needn't show every extreme that they name: `pattern`: within one block row and column tile the non-negative entries are distinct; every block row holds 0 to 2 stored blocks in each column tile, and 2 in some. `density`: empty slots hold zero blocks.
All inputs are finite; a program needn't handle non-finite values.
Results may differ from a plain program's by a relative error of at most 0.001.
Values may be sent and summed in bfloat16 or wider, within the bound.
A program may use at most 192 MiB of HBM per device.

v0:
```python
import jax
import jax.numpy as jnp
from jax import lax
from jax.sharding import PartitionSpec as P


def on_device(density, pattern):
    rows = density.shape[0]
    half = density.shape[2]
    size = density.shape[3]
    layered = (
        lax.all_gather(density, "layer", axis=2, tiled=True),
        lax.all_gather(pattern, "layer", axis=2, tiled=True),
    )
    strip_vals, strip_cols = (
        lax.all_gather(layered[0], "row", axis=0, tiled=True),
        lax.all_gather(layered[1], "row", axis=0, tiled=True),
    )
    b_vals = strip_vals[:, 0]
    b_cols = strip_cols[:, 0]
    order = b_vals.shape[0]
    width = order // lax.axis_size("col")
    out_cols = lax.dynamic_slice_in_dim(b_cols, lax.axis_index("row") * rows, rows, 0)
    p_vals = lax.all_gather(density, "col", axis=1, tiled=True)
    p_cols = lax.all_gather(pattern, "col", axis=1, tiled=True)
    count = p_cols.shape[1]
    owner = jnp.arange(count, dtype=jnp.int32)[None, :, None] * width
    inner = jnp.clip(owner + p_cols, 0, order - 1).reshape(rows, count * half)
    a_vals = p_vals.reshape(rows, count * half, size, size)
    fetched = jnp.take(b_vals, inner, axis=0)
    fetched_cols = jnp.take(b_cols, inner, axis=0)
    match = (fetched_cols[:, :, None, :] == out_cols[:, None, :, None]).astype(jnp.bfloat16)
    chosen = jnp.einsum(
        "iqsb,iqbxy->iqsxy", match, fetched, preferred_element_type=jnp.float32
    ).astype(jnp.bfloat16)
    partial_sum = jnp.einsum("iqxy,iqsyz->isxz", a_vals, chosen, preferred_element_type=jnp.float32)
    whole_sum = lax.psum(partial_sum, "layer")
    mine = lax.dynamic_slice_in_dim(whole_sum, lax.axis_index("layer") * half, half, 1)
    full = mine[:, None]
    squared = full.astype(jnp.bfloat16)
    raised = (2.0 * density.astype(jnp.float32) - full).astype(jnp.bfloat16)
    return (squared, raised)


def solution(mesh):
    placed = (P("row", "col", "layer", None, None), P("row", "col", "layer"))
    return jax.shard_map(
        on_device,
        mesh=mesh,
        in_specs=placed,
        out_specs=(P("row", "col", "layer", None, None), P("row", "col", "layer", None, None)),
        check_vma=False,
    )
```

profile of v0, /device:TPU:2, one launch (start us, length us, event | category | flops | bytes accessed | tf_op | source)
XLA Modules:
  0.0 499.9 jit_solution(16046760701412596642)
XLA Ops:
  7.2 0.0 all-gather.4.cloned.1.call-start
  7.2 0.7 all-gather.4.cloned.1.call-update
  7.9 0.0 all-gather.6.cloned.1.call-start
  7.9 43.1 %all-gather.4.cloned.1.call-done = bf16[64,1,2,64,64]{4,3,2,1,0:T(8,128)(2,1)} async-done(((bf16[64,1,1,64,64]{4,3,2,1,0:T(8,128)(2,1)}), bf16[64,1,2,64,64]{4,3,2,1,0:T(8,128)(2,1)}) %all-gather.4.cloned.1.call-update) | async-done | bytes 1048592 | tf_op jit(solution)/shard_map/all_gather | solution.py:12
  51.1 0.0 all-gather.6.cloned.1.call-update
  51.1 0.0 all-gather.8.cloned.1.call-start
  51.1 0.7 all-gather.8.cloned.1.call-update
  51.8 0.0 all-reduce.2.cloned.1.call-start
  51.9 4.4 all_gather.19
  56.2 0.1 copy.38
  56.3 43.3 %all_gather.18 = s32[64,16,1]{0,2,1:T(1,128)S(1)} all-gather(s32[64,1,1]{0,2,1:T(1,128)} %param.3), channel_id=1, replica_groups=mesh['layer'=2,'row'=8,'col'=16] {'col'}, dimensions={1}, use_global_device_ids=true | all-gather | bytes 4352 | tf_op jit(solution)/shard_map/all_gather | solution.py:25
  99.6 0.1 and_bitcast_fusion
  99.7 0.1 copy.39
  99.8 0.1 reshape.40
  99.9 0.1 copy.36
  100.0 13.3 %all_gather.20 = s32[512,1,2]{2,0,1:T(8,128)S(1)} all-gather(s32[64,1,2]{2,0,1:T(8,128)S(1)} %copy.38), channel_id=1, replica_groups=mesh['layer'=2,'row'=8,'col'=16] {'row'}, dimensions={0}, use_global_device_ids=true | all-gather | bytes 4608 | tf_op jit(solution)/shard_map/all_gather | solution.py:17
  113.2 2.8 gather_fusion
  116.1 0.2 broadcast_select_fusion.2
  116.3 25.2 %all-gather.6.cloned.1.call-done = bf16[512,1,2,64,64]{4,3,2,1,0:T(8,128)(2,1)} async-done(((bf16[64,1,2,64,64]{4,3,2,1,0:T(8,128)(2,1)}), bf16[512,1,2,64,64]{4,3,2,1,0:T(8,128)(2,1)}) %all-gather.6.cloned.1.call-update) | async-done | bytes 8388624 | tf_op jit(solution)/shard_map/all_gather | solution.py:16
  141.5 26.6 %gather_fusion.1 = bf16[1024,2,64,64]{3,2,1,0:T(8,128)(2,1)} fusion(bf16[512,2,64,64]{3,2,1,0:T(8,128)(2,1)} %bitcast.50, s32[1024]{0:T(1024)S(1)} %broadcast_clamp_fusion), kind=kCustom, calls=%fused_computation.1 | custom fusion | bytes 33558528 | tf_op jit(solution)/shard_map/jit(_take)/gather | solution.py:30
  168.1 64.9 %convolution_convert_fusion = bf16[64,16,2,64,64]{4,2,3,1,0:T(2,128)(2,1)} fusion(pred[64,16]{1,0:T(8,128)(4,1)S(1)} %copy.36, bf16[64,16,2,64,64]{4,3,2,1,0:T(8,128)(2,1)} %bitcast.51, s32[64,2]{1,0:T(8,128)S(1)} %dynamic-slice_bitcast_fusion, s32[64,16,2]{2,1,0:T(8,128)S(1)} %broadcast_select_fusion.2), kind=kOutput, calls=%fused_computation.3 | convolution fusion | flops 50335744 | bytes 33564160 | tf_op jit(solution)/shard_map/iqsb,iqbxy->iqsxy/dot_general | solution.py:33
  233.0 0.0 copy-start
  233.0 114.5 %all-gather.8.cloned.1.call-done = bf16[64,16,1,64,64]{4,3,1,0,2:T(8,128)(2,1)} async-done(((bf16[64,1,1,64,64]{4,3,1,0,2:T(8,128)(2,1)}), bf16[64,16,1,64,64]{4,3,1,0,2:T(8,128)(2,1)}) %all-gather.8.cloned.1.call-update) | async-done | bytes 8388624 | tf_op jit(solution)/shard_map/all_gather | solution.py:24
  347.6 21.0 %fusion.4 = f32[64,2,64,64]{2,3,1,0:T(8,128)} fusion(bf16[64,16,1,64,64]{4,3,1,0,2:T(8,128)(2,1)} %all-gather.8.cloned.1.call-done, bf16[64,16,2,64,64]{4,2,3,1,0:T(2,128)(2,1)} %convolution_convert_fusion), kind=kOutput, calls=%fused_computation.8 | convolution fusion | flops 1073741824 | bytes 27262976 | tf_op jit(solution)/shard_map/iqxy,iqsyz->isxz/dot_general | solution.py:36
  368.5 0.0 all-reduce.2.cloned.1.call-update
  368.6 117.2 %all-reduce.2.cloned.1.call-done = f32[64,2,64,64]{2,3,1,0:T(8,128)} async-done(((f32[64,2,64,64]{2,3,1,0:T(8,128)}), f32[64,2,64,64]{2,3,1,0:T(8,128)}) %all-reduce.2.cloned.1.call-update) | async-done | bytes 2097168 | tf_op jit(solution)/shard_map/psum | solution.py:37
  485.7 3.2 constant_dynamic-slice_fusion
  488.9 1.9 copy.46
  490.8 0.0 copy-done
  490.9 1.3 fusion.10
  492.2 1.2 fusion.11
  (3 shorter events, 0.0 us)
Async XLA Ops:
  7.2 43.9 %all-gather.4.cloned.1.call-start = ((), (), s32[]{:S(2)}) async-start(), calls=%async_computation | async-start | bytes 3145728 | tf_op jit(solution)/shard_map/all_gather | solution.py:12
  7.9 133.6 %all-gather.6.cloned.1.call-start = ((), (), s32[]{:S(2)}) async-start(), calls=%async_computation.1 | async-start | bytes 18874368 | tf_op jit(solution)/shard_map/all_gather | solution.py:16
  51.1 296.5 %all-gather.8.cloned.1.call-start = ((), (), s32[]{:S(2)}) async-start(), calls=%async_computation.2 | async-start | bytes 17825792 | tf_op jit(solution)/shard_map/all_gather | solution.py:24
  51.8 433.9 %all-reduce.2.cloned.1.call-start = ((), (), s32[]{:S(2)}) async-start(), calls=%async_computation.3 | async-start | bytes 8388608 | tf_op jit(solution)/shard_map/psum | solution.py:37
  233.0 257.8 %copy-start = (bf16[64,1,1,64,64]{4,3,2,1,0:T(8,128)(2,1)S(1)}, bf16[64,1,1,64,64]{4,3,2,1,0:T(8,128)(2,1)}, u32[]{:S(2)}) copy-start(bf16[64,1,1,64,64]{4,3,2,1,0:T(8,128)(2,1)} %param.2) | copy-start | bytes 1572868
Sparse Core Ops, SparseCore 0:
  9.8 41.2 all-gather.3
  52.9 88.5 all-gather.5
  144.0 203.4 all-gather.7
  368.7 117.0 all-reduce.1
where the time goes:
time: 501 us; the launch traced here: 500 us
  waiting for transfers between devices  301 us (60%)
  matrix products  85.9 us (17%)
  blocking collectives  60.9 us (12%)
  local copies, waits for them, and re-layouts  34.8 us (7%)
  between operations  13.8 us (3%)
    psum x1, waiting for transfers between devices, on_device(): whole_sum = lax.psum(partial_sum, 'layer')  117 us
    all_gather x1, waiting for transfers between devices, on_device(): p_vals = lax.all_gather(density, 'col', axis=1, tiled=True)  115 us
    dot_general x1, matrix products, on_device(): jnp.einsum('iqsb,iqbxy->iqsxy', match, fetched, preferred_element_type=jn...  64.9 us
    all_gather x1, blocking collectives, on_device(): p_cols = lax.all_gather(pattern, 'col', axis=1, tiled=True)  43.3 us
    all_gather x1, waiting for transfers between devices, on_device(): lax.all_gather(density, 'layer', axis=2, tiled=True)  43.1 us
    gather x1, local copies, waits for them, and re-layouts, on_device(): fetched = jnp.take(b_vals, inner, axis=0)  26.6 us
    all_gather x1, waiting for transfers between devices, on_device(): lax.all_gather(layered[0], 'row', axis=0, tiled=True)  25.2 us
    dot_general x1, matrix products, on_device(): jnp.einsum('iqxy,iqsyz->isxz', a_vals, chosen, preferred_element_type=jnp...  21 us
  transfers between devices with their start and end apart: 4, of which 4 were waited for; matrix products, arithmetic and copies ran while one was open for 19% of the time, Pallas kernels for 0%

commit v1 on v0

v1 whole, which is shorter than its diff:
```python
import jax
import jax.numpy as jnp
from jax import lax
from jax.experimental import pallas as pl
from jax.experimental.pallas import tpu as pltpu
from jax.sharding import PartitionSpec as P

MESH = pl.DeviceIdType.MESH
F32 = jnp.float32
BF16 = jnp.bfloat16

B = 64
W = 2 * B
HALF = 32
BODY = HALF * B
PAY = BODY + HALF
UNIT = PAY // 2
TILES = 16
YS, ZS, XS = 4, 4, 4


def lanes(rows):
    return lax.broadcasted_iota(jnp.int32, (rows, W), 1)


def gather_kernel(d_ref, p_ref, a_ref, b_ref, slots, merged,
                  ex_s, ex_r, z_s, z_r, y_s, y_r, f_s, f_r, x_s, x_r, t_s, t_r, l_s):
    layer, row, col = lax.axis_index("layer"), lax.axis_index("row"), lax.axis_index("col")
    x, core = row // 2, row % 2
    y, z = col // ZS, col % ZS
    twin = x * 2 + 1 - core

    def at_z(d):
        return y * ZS + (z + d) % ZS

    def at_y(d):
        return ((y + d) % YS) * ZS + z

    def at_x(d):
        return ((x + d) % XS) * 2 + core

    peers = [{"layer": 1 - layer}, {"row": twin}]
    peers += [{"col": at_z(d)} for d in (1, 2, 3)]
    peers += [{"col": at_y(d)} for d in (1, 3)]
    peers += [{"row": at_x(d)} for d in (1, 2, 3)]
    barrier = pltpu.get_barrier_semaphore()
    for peer in peers:
        pl.semaphore_signal(barrier, inc=1, device_id=peer, device_id_type=MESH)

    @pl.loop(0, HALF)
    def _(j):
        slots[layer, pl.ds(pl.multiple_of(j * B, B), B), :] = jnp.concatenate(
            [d_ref[j], d_ref[j + HALF]], axis=1
        )

    number = p_ref[...].astype(F32)
    lane = lax.broadcasted_iota(jnp.int32, (HALF, B), 1)
    sub = lax.broadcasted_iota(jnp.int32, (HALF, B), 0)
    low = jnp.sum(jnp.where(lane == sub, number, 0.0), axis=1, keepdims=True)
    high = jnp.sum(jnp.where(lane == sub + HALF, number, 0.0), axis=1, keepdims=True)
    slots[layer, pl.ds(BODY, HALF), :] = jnp.where(lanes(HALF) < B, low, high).astype(BF16)

    pl.semaphore_wait(barrier, len(peers))

    def part(u):
        return pl.ds(u * UNIT, UNIT)

    sends, pending = [], []

    def send(src, dst, ssem, rsem, peer):
        copy = pltpu.make_async_remote_copy(
            src_ref=src, dst_ref=dst, send_sem=ssem, recv_sem=rsem, device_id=peer, device_id_type=MESH
        )
        copy.start()
        sends.append(copy)
        return copy

    ex = [
        send(slots.at[layer, part(u)], slots.at[layer, part(u)], ex_s.at[u], ex_r.at[u], {"layer": 1 - layer})
        for u in (0, 1)
    ]

    def arrived(ref, ssem, rsem):
        pltpu.make_async_remote_copy(
            src_ref=ref, dst_ref=ref, send_sem=ssem, recv_sem=rsem, device_id={"layer": 1 - layer},
            device_id_type=MESH,
        ).wait_recv()

    mine = merged.at[layer]
    local = []
    for u in (0, 1):
        arrived(slots.at[1 - layer, part(u)], ex_s.at[u], ex_r.at[u])

        @pl.loop(0, UNIT // 16)
        def _(i):
            at = pl.ds(pl.multiple_of(u * UNIT + i * 16, 16), 16)
            one, two = slots[0, at, :], slots[1, at, :]
            left = lanes(16) < B
            swap_one = jnp.concatenate([one[:, B:], one[:, :B]], axis=1)
            swap_two = jnp.concatenate([two[:, B:], two[:, :B]], axis=1)
            merged[0, at, :] = jnp.where(left, one, swap_two)
            merged[1, at, :] = jnp.where(left, swap_one, two)

        for k, d in enumerate((1, 3)):
            send(mine.at[part(u)], a_ref.at[col, part(u)], y_s.at[0, k, u], y_r.at[0, k, u], {"col": at_y(d)})
        for d in (1, 3, 2):
            send(mine.at[part(u)], a_ref.at[col, part(u)], z_s.at[d - 1, u], z_r.at[d - 1, u], {"col": at_z(d)})
        for h in (0, 1):
            send(merged.at[h, part(u)], b_ref.at[2 * row + h, part(u)], t_s.at[h, u], t_r.at[h, u], {"row": twin})
        for d in (1, 3, 2):
            send(merged.at[core, part(u)], b_ref.at[2 * row + core, part(u)],
                 x_s.at[d - 1, 0, u], x_r.at[d - 1, 0, u], {"row": at_x(d)})
        for h in (0, 1):
            local.append(pltpu.make_async_copy(merged.at[h, part(u)], b_ref.at[2 * row + h, part(u)], l_s.at[h, u]))
        local.append(pltpu.make_async_copy(mine.at[part(u)], a_ref.at[col, part(u)], l_s.at[2, u]))
        for copy in local[-3:]:
            copy.start()

    def twin_in(h, u):
        ref = b_ref.at[2 * twin + h, part(u)]
        arrived(ref, t_s.at[h, u], t_r.at[h, u])

    def on_z(d, u):
        ref = a_ref.at[y * ZS + (z + ZS - d) % ZS, part(u)]
        arrived(ref, z_s.at[d - 1, u], z_r.at[d - 1, u])
        for k, e in enumerate((1, 3)):
            send(ref, ref, y_s.at[d, k, u], y_r.at[d, k, u], {"col": at_y(e)})

    def on_y(d, k, u):
        ref = a_ref.at[((y + (3, 1)[k]) % YS) * ZS + (z + ZS - d) % ZS, part(u)]
        arrived(ref, y_s.at[d, k, u], y_r.at[d, k, u])
        if k == u:
            send(ref, ref, f_s.at[d, k], f_r.at[d, k], {"col": at_y((1, 3)[k])})

    def on_f(d, k):
        ref = a_ref.at[((y + 2) % YS) * ZS + (z + ZS - d) % ZS, part(k)]
        arrived(ref, f_s.at[d, k], f_r.at[d, k])

    def on_x(d, p, u):
        there = ((x + XS - d) % XS) * 2 + (core if p == 0 else 1 - core)
        ref = b_ref.at[2 * there + core, part(u)]
        arrived(ref, x_s.at[d - 1, p, u], x_r.at[d - 1, p, u])
        n = 2 + (d - 1) * 2 + p
        send(ref, ref, t_s.at[n, u], t_r.at[n, u], {"row": twin})

    for u in (0, 1):
        twin_in(0, u)
        twin_in(1, u)
        for d in (1, 3, 2):
            ref = b_ref.at[2 * twin + core, part(u)]
            send(ref, ref, x_s.at[d - 1, 1, u], x_r.at[d - 1, 1, u], {"row": at_x(d)})
    for u in (0, 1):
        on_y(0, 0, u)
        on_y(0, 1, u)
        on_z(1, u)
        on_z(3, u)
    for u in (0, 1):
        on_x(1, 0, u)
        on_x(3, 0, u)
        on_z(2, u)
    for u in (0, 1):
        for d in (1, 3):
            on_y(d, 0, u)
            on_y(d, 1, u)
        on_x(1, 1, u)
        on_x(3, 1, u)
        on_x(2, 0, u)
        on_x(2, 1, u)
    for u in (0, 1):
        on_y(2, 0, u)
        on_y(2, 1, u)
    for d in (0, 1, 3, 2):
        on_f(d, 0)
        on_f(d, 1)
    for d in (1, 2, 3):
        for p in (0, 1):
            there = ((x + XS - d) % XS) * 2 + (1 - core if p == 0 else core)
            n = 2 + (d - 1) * 2 + p
            for u in (0, 1):
                arrived(b_ref.at[2 * there + 1 - core, part(u)], t_s.at[n, u], t_r.at[n, u])
    for copy in sends:
        copy.wait_send()
    for copy in local:
        copy.wait()


def gather(d, p):
    wide = jax.ShapeDtypeStruct((TILES, PAY, W), BF16)
    dma = pltpu.SemaphoreType.DMA
    return pl.pallas_call(
        gather_kernel,
        out_shape=(wide, wide),
        in_specs=[pl.BlockSpec(memory_space=pltpu.VMEM)] * 2,
        out_specs=(pl.BlockSpec(memory_space=pl.ANY),) * 2,
        scratch_shapes=[
            pltpu.VMEM((2, PAY, W), BF16),
            pltpu.VMEM((2, PAY, W), BF16),
            dma((2,)), dma((2,)),
            dma((3, 2)), dma((3, 2)),
            dma((4, 2, 2)), dma((4, 2, 2)),
            dma((4, 2)), dma((4, 2)),
            dma((3, 2, 2)), dma((3, 2, 2)),
            dma((8, 2)), dma((8, 2)),
            dma((3, 2)),
        ],
        compiler_params=pltpu.CompilerParams(
            collective_id=0, has_side_effects=True, vmem_limit_bytes=12 << 20
        ),
        name="gather",
    )(d, p)


def multiply_kernel(a_ref, b_ref, o_ref, acc, codes, scalars, sem):
    col = lax.axis_index("col")
    sub = lax.broadcasted_iota(jnp.int32, (HALF, W), 0)
    place = lanes(HALF) % B

    def in_row(block):
        return jnp.sum(jnp.where(place == sub, block, 0.0), axis=0, keepdims=True)

    def turn(v):
        return jnp.concatenate([v[:, B:], v[:, :B]], axis=1)

    want = in_row(a_ref[col, pl.ds(BODY, HALF), :].astype(F32))
    want_turned = turn(want)
    right = lanes(1) >= B
    used = lanes(1) % B < HALF
    for t in range(TILES):
        inner = in_row(a_ref[t, pl.ds(BODY, HALF), :].astype(F32))
        table = b_ref[t, pl.ds(BODY, HALF), :].astype(F32)
        hot = inner == sub.astype(F32)
        own = jnp.sum(jnp.where(hot, table, 0.0), axis=0, keepdims=True)
        other = jnp.sum(jnp.where(hot, turn(table), 0.0), axis=0, keepdims=True)
        live = used & (inner >= 0)

        def same(u, v):
            return jnp.where(live & (u == v) & (v >= 0), 1, 0)

        f0, f1 = same(own, want), same(other, want)
        f2, f3 = same(own, want_turned), same(other, want_turned)
        flags = (
            jnp.where(right, f3, f0) + 2 * jnp.where(right, f0, f3)
            + 4 * jnp.where(right, f2, f1) + 8 * jnp.where(right, f1, f2)
        )
        codes[pl.ds(t, 1), :] = jnp.where(flags > 0, flags + 16 * inner.astype(jnp.int32), 0)
    copy = pltpu.make_async_copy(codes, scalars, sem)
    copy.start()

    @pl.loop(0, HALF)
    def _(j):
        acc[j] = jnp.zeros((B, W), F32)

    copy.wait()

    @pl.loop(0, TILES)
    def _(t):
        for s in (0, 1):
            @pl.loop(0, HALF, unroll=8)
            def _(j):
                code = scalars[t, s * B + j]

                @pl.when(code > 0)
                def _():
                    k = code // 16
                    left = lanes(1) < B

                    def pick(bit_left, bit_right):
                        return jnp.where(left, (code // bit_left) % 2, (code // bit_right) % 2).astype(F32)

                    v = b_ref[t, pl.ds(pl.multiple_of(k * B, B), B), :].astype(F32)
                    w = (v * pick(1, 2) + turn(v) * pick(4, 8)).astype(BF16)
                    a = a_ref[t, pl.ds(pl.multiple_of(j * B, B), B), :]
                    acc[j] += jnp.dot(a[:, s * B:(s + 1) * B], w, preferred_element_type=F32)

    @pl.loop(0, HALF)
    def _(j):
        full = acc[j]
        mine = a_ref[col, pl.ds(pl.multiple_of(j * B, B), B), :].astype(F32)
        squared = full
        raised = 2.0 * mine - full
        left = lanes(B) < B
        o_ref[0, j] = jnp.where(left, squared, turn(raised)).astype(BF16)
        o_ref[1, j] = jnp.where(left, turn(squared), raised).astype(BF16)


def multiply(a, b):
    return pl.pallas_call(
        multiply_kernel,
        out_shape=jax.ShapeDtypeStruct((2, HALF, B, W), BF16),
        in_specs=[pl.BlockSpec(memory_space=pltpu.VMEM)] * 2,
        out_specs=pl.BlockSpec(memory_space=pltpu.VMEM),
        scratch_shapes=[
            pltpu.VMEM((HALF, B, W), F32),
            pltpu.VMEM((TILES, W), jnp.int32),
            pltpu.SMEM((TILES, W), jnp.int32),
            pltpu.SemaphoreType.DMA,
        ],
        compiler_params=pltpu.CompilerParams(vmem_limit_bytes=32 << 20),
        name="multiply",
    )(a, b)


CUTS = 4


def swap_kernel(o_ref, sq_ref, ra_ref, got, s_sem, r_sem):
    layer = lax.axis_index("layer")
    other = {"layer": 1 - layer}
    barrier = pltpu.get_barrier_semaphore()
    pl.semaphore_signal(barrier, inc=1, device_id=other, device_id_type=MESH)
    pl.semaphore_wait(barrier, 1)
    size = HALF // CUTS
    copies = []
    for n in range(CUTS):
        at = pl.ds(n * size, size)
        copy = pltpu.make_async_remote_copy(
            src_ref=o_ref.at[1 - layer, at], dst_ref=got.at[at], send_sem=s_sem.at[n], recv_sem=r_sem.at[n],
            device_id=other, device_id_type=MESH,
        )
        copy.start()
        copies.append(copy)

    @pl.loop(0, HALF)
    def _(j):
        both = o_ref[layer, j]
        sq_ref[layer * HALF + j] = both[:, :B]
        ra_ref[layer * HALF + j] = both[:, B:]

    for n, copy in enumerate(copies):
        copy.wait_recv()

        @pl.loop(n * size, (n + 1) * size)
        def _(j):
            both = got[j]
            sq_ref[(1 - layer) * HALF + j] = both[:, :B]
            ra_ref[(1 - layer) * HALF + j] = both[:, B:]

    for copy in copies:
        copy.wait_send()


def swap(o):
    out = jax.ShapeDtypeStruct((2 * HALF, B, B), BF16)
    return pl.pallas_call(
        swap_kernel,
        out_shape=(out, out),
        in_specs=[pl.BlockSpec(memory_space=pltpu.VMEM)],
        out_specs=(pl.BlockSpec(memory_space=pltpu.VMEM),) * 2,
        scratch_shapes=[
            pltpu.VMEM((HALF, B, W), BF16),
            pltpu.SemaphoreType.DMA((CUTS,)),
            pltpu.SemaphoreType.DMA((CUTS,)),
        ],
        compiler_params=pltpu.CompilerParams(
            collective_id=1, has_side_effects=True, vmem_limit_bytes=12 << 20
        ),
        name="swap",
    )(o)


def on_device(density, pattern):
    a, b = gather(density.reshape(2 * HALF, B, B), pattern.reshape(1, 2 * HALF))
    squared, raised = swap(multiply(a, b))
    return squared.reshape(density.shape), raised.reshape(density.shape)


def solution(mesh):
    placed = (P("row", "col", "layer", None, None), P("row", "col", "layer"))
    return jax.shard_map(
        on_device,
        mesh=mesh,
        in_specs=placed,
        out_specs=(P("row", "col", "layer", None, None), P("row", "col", "layer", None, None)),
        check_vma=False,
    )
```

time: 501 us -> 133 us (0.27)
  waiting for transfers between devices: 301 us -> 0 us
  Pallas kernels: 0 us -> 129 us
  matrix products: 85.9 us -> 0 us
  blocking collectives: 60.9 us -> 0 us
  local copies, waits for them, and re-layouts: 34.8 us -> 3.81 us
  between operations: 13.8 us -> 0.66 us
    all_gather x3 -> x0, waiting for transfers between devices: 183 us -> none  [the longest x1 115 us: on_device(): p_vals = lax.all_gather(density, 'col', axis=1, tiled=True)]
    pallas_call x0 -> x3, Pallas kernels: none -> 129 us  [the longest x1 98.8 us: gather(): pl.pallas_call(gather_kernel, out_shape=(wide, wide), in_specs=[pl.BlockS...]
    psum x1 -> x0, waiting for transfers between devices: 117 us -> none  [on_device(): whole_sum = lax.psum(partial_sum, 'layer')]
    dot_general x2 -> x0, matrix products: 85.9 us -> none  [the longest x1 64.9 us: on_device(): jnp.einsum('iqsb,iqbxy->iqsxy', match, fetched, preferred_element_type=jn...]
    all_gather x3 -> x0, blocking collectives: 60.9 us -> none  [the longest x1 43.3 us: on_device(): p_cols = lax.all_gather(pattern, 'col', axis=1, tiled=True)]
    gather x2 -> x0, local copies, waits for them, and re-layouts: 29.4 us -> none  [the longest x1 26.6 us: on_device(): fetched = jnp.take(b_vals, inner, axis=0)]
    dynamic_slice x2 -> x0, local copies, waits for them, and re-layouts: 5.09 us -> none  [on_device(): lax.dynamic_slice_in_dim(whole_sum, lax.axis_index('layer') * half, half, 1)]
  transfers between devices with their start and end apart: 4 -> 0, of which waited for: 4 -> 0; matrix products, arithmetic and copies ran while one was open for 19% -> 0% of each run, Pallas kernels for 0% -> 0%
where the time goes in v1:
time: 133 us
  Pallas kernels  129 us (97%)
  local copies, waits for them, and re-layouts  3.81 us (3%)
    pallas_call x1, Pallas kernels, gather(): pl.pallas_call(gather_kernel, out_shape=(wide, wide), in_specs=[pl.BlockS...  98.8 us
    pallas_call x1, Pallas kernels, multiply(): pl.pallas_call(multiply_kernel, out_shape=jax.ShapeDtypeStruct((2, HALF,...  19.8 us
    pallas_call x1, Pallas kernels, swap(): pl.pallas_call(swap_kernel, out_shape=(out, out), in_specs=[pl.BlockSpec(...  10 us
    unnamed x6, local copies, waits for them, and re-layouts  3.81 us

profile of v1, /device:TPU:2, one launch (start us, length us, event | category | flops | bytes accessed | tf_op | source)
XLA Modules:
  0.0 133.1 jit_solution(8279023253766368292)
XLA Ops:
  0.6 0.0 copy-start
  0.6 1.2 copy-done
  1.9 0.0 copy-start.1
  1.9 0.7 copy-done.1
  2.5 98.8 %gather.1 = (bf16[16,2080,128]{2,1,0:T(8,128)(2,1)S(1)}, bf16[16,2080,128]{2,1,0:T(8,128)(2,1)S(1)}) custom-call(bf16[64,64,64]{2,1,0:T(8,128)(2,1)S(1)} %bitcast.8, s32[1,64]{1,0:T(1,128)S(1)} %bitcast.11), custom_call_target="tpu_custom_call" | custom-call | tf_op jit(solution)/shard_map/gather/pallas_call | solution.py:190
  101.3 19.8 %multiply.1.o_ref = bf16[2,32,64,128]{3,2,1,0:T(8,128)(2,1)S(1)} custom-call(bf16[16,2080,128]{2,1,0:T(8,128)(2,1)S(1)} %get-tuple-element.6.a_ref, bf16[16,2080,128]{2,1,0:T(8,128)(2,1)S(1)} %get-tuple-element.7.b_ref), custom_call_target="tpu_custom_call" | custom-call | tf_op jit(solution)/shard_map/multiply/pallas_call | solution.py:287
  121.2 10.0 %swap.1 = (bf16[64,64,64]{2,1,0:T(8,128)(2,1)S(1)}, bf16[64,64,64]{2,1,0:T(8,128)(2,1)S(1)}) custom-call(bf16[2,32,64,128]{3,2,1,0:T(8,128)(2,1)S(1)} %multiply.1.o_ref), custom_call_target="tpu_custom_call" | custom-call | tf_op jit(solution)/shard_map/swap/pallas_call | solution.py:344
  131.2 1.0 copy.8
  132.1 1.0 copy.9
Async XLA Ops:
  0.6 1.2 copy-start
  1.9 0.7 copy-start.1

commit v2 on v1

v2 whole, which is shorter than its diff:
```python
import jax
import jax.numpy as jnp
from jax import lax
from jax.experimental import pallas as pl
from jax.experimental.pallas import tpu as pltpu
from jax.sharding import PartitionSpec as P

MESH = pl.DeviceIdType.MESH
F32 = jnp.float32
BF16 = jnp.bfloat16

B = 64
W = 2 * B
HALF = 32
PAIRS = HALF // 2
BODY = PAIRS * B
UNIT = BODY + PAIRS
TILES = 16
YS, ZS, XS = 4, 4, 4


def lanes(rows):
    return lax.broadcasted_iota(jnp.int32, (rows, W), 1)


def gather_kernel(d_ref, p_ref, a_ref, b_ref,
                  e_s, e_r, z_s, z_r, y_s, y_r, f_s, f_r, g_s, g_r, x_s, x_r, t_s, t_r, l_s):
    layer, row, col = lax.axis_index("layer"), lax.axis_index("row"), lax.axis_index("col")
    x, core = row // 2, row % 2
    y, z = col // ZS, col % ZS
    twin = x * 2 + 1 - core
    step, away = 1 + 2 * core, 3 - 2 * layer

    def at_z(d):
        return y * ZS + (z + d) % ZS

    def at_y(d):
        return ((y + d) % YS) * ZS + z

    def at_x(d):
        return ((x + d) % XS) * 2 + core

    other = {"layer": 1 - layer}
    aside = {"layer": 1 - layer, "col": at_z(away)}
    peers = [other, aside, {"row": twin}]
    peers += [{"col": at_z(d)} for d in (1, 3)]
    peers += [{"col": at_y(d)} for d in (1, 3)]
    peers += [{"row": at_x(d)} for d in (1, 2, 3)]
    barrier = pltpu.get_barrier_semaphore()
    for peer in peers:
        pl.semaphore_signal(barrier, inc=1, device_id=peer, device_id_type=MESH)

    number = p_ref[...].astype(F32)
    lane = lax.broadcasted_iota(jnp.int32, (PAIRS, B), 1)
    sub = lax.broadcasted_iota(jnp.int32, (PAIRS, B), 0)

    def entry(first):
        return jnp.sum(jnp.where(lane == sub + first, number, 0.0), axis=1, keepdims=True)

    for h in (0, 1):
        @pl.loop(0, PAIRS)
        def _(j):
            b_ref[2 * row + h, layer, pl.ds(pl.multiple_of(j * B, B), B), :] = jnp.concatenate(
                [d_ref[h * HALF + j], d_ref[h * HALF + PAIRS + j]], axis=1
            )

        b_ref[2 * row + h, layer, pl.ds(BODY, PAIRS), :] = jnp.where(
            lanes(PAIRS) < B, entry(h * HALF), entry(h * HALF + PAIRS)
        ).astype(BF16)

    pl.semaphore_wait(barrier, len(peers))

    sends, local = [], []

    def send(src, dst, ssem, rsem, peer):
        copy = pltpu.make_async_remote_copy(
            src_ref=src, dst_ref=dst, send_sem=ssem, recv_sem=rsem, device_id=peer, device_id_type=MESH
        )
        copy.start()
        sends.append(copy)

    def arrived(ref, ssem, rsem):
        pltpu.make_async_remote_copy(
            src_ref=ref, dst_ref=ref, send_sem=ssem, recv_sem=rsem, device_id=other, device_id_type=MESH
        ).wait_recv()

    offset = (0, 4 - step, step, 0, away, 4 - away, 2, 2)
    whose = (layer, layer, layer, 1 - layer, 1 - layer, 1 - layer, 1 - layer, layer)

    def a_at(dy, n):
        return a_ref.at[((y + dy) % YS) * ZS + (z + offset[n]) % ZS, whose[n]]

    def b_at(there, h, s):
        return b_ref.at[2 * there + h, s]

    mine, theirs = b_at(row, layer, layer), b_at(row, 1 - layer, layer)

    def sense(n):
        return 1 + 2 * ((n + core) % 2)

    def to_y(src, n):
        for k, d in enumerate((sense(n), 4 - sense(n))):
            send(src, a_at(0, n), y_s.at[n, k], y_r.at[n, k], {"col": at_y(d)})

    def to_x(src, h, own):
        n = h * 2 + own
        for d in (1, 3, 2):
            send(src, src, x_s.at[n, d - 1], x_r.at[n, d - 1], {"row": at_x(d)})

    def to_twin(src, n):
        send(src, src, t_s.at[n], t_r.at[n], {"row": twin})

    def keep(src, n):
        copy = pltpu.make_async_copy(src, a_at(0, n), l_s.at[n // 3])
        copy.start()
        local.append(copy)

    def pass_far(ref, m):
        send(ref, ref, g_s.at[m], g_r.at[m], {"col": at_z(step)})

    to_y(mine, 0)
    send(theirs, theirs, z_s.at[3], z_r.at[3], other)
    send(mine, a_at(0, 0), z_s.at[1], z_r.at[1], {"col": at_z(step)})
    send(theirs, a_at(0, 0), z_s.at[4], z_r.at[4], aside)
    send(mine, a_at(0, 0), z_s.at[2], z_r.at[2], {"col": at_z(4 - step)})
    to_x(mine, 0, 0)
    to_x(theirs, 1, 0)
    to_twin(mine, 0)
    to_twin(theirs, 2)
    keep(mine, 0)

    def on_z(n):
        if n == 3:
            ref = b_at(row, layer, 1 - layer)
            arrived(ref, z_s.at[n], z_r.at[n])
            send(ref, a_at(0, 3), z_s.at[5], z_r.at[5], {"col": at_z(away)})
        else:
            ref = a_at(0, n)
            arrived(ref, z_s.at[n], z_r.at[n])
            if n == 1:
                pass_far(ref, 0)
            if n == 4:
                send(ref, ref, z_s.at[6], z_r.at[6], {"col": at_z(4 - away)})
        to_y(ref, n)
        if n == 3:
            to_x(ref, 0, 1)
            to_twin(ref, 1)
            keep(ref, 3)

    def on_y(n, k):
        d = (4 - sense(n), sense(n))[k]
        ref = a_at(d, n)
        arrived(ref, y_s.at[n, k], y_r.at[n, k])
        if n == 1:
            pass_far(ref, 1 + k)
        if k == 0:
            send(ref, ref, f_s.at[n], f_r.at[n], {"col": at_y(sense(n))})

    def on_f(n):
        ref = a_at(2, n)
        arrived(ref, f_s.at[n], f_r.at[n])
        if n == 1:
            pass_far(ref, 3)

    def on_far(m):
        arrived(a_at((0, 4 - sense(1), sense(1), 2)[m], 7), g_s.at[m], g_r.at[m])

    def on_x(d, h, own):
        there = ((x + XS - d) % XS) * 2 + core
        ref = b_at(there, (layer, 1 - layer)[h], (layer, 1 - layer)[own])
        n = h * 2 + own
        arrived(ref, x_s.at[n, d - 1], x_r.at[n, d - 1])
        to_twin(ref, 4 + n * 3 + d - 1)

    on_z(3)
    on_z(1)
    on_y(0, 0)
    on_z(4)
    send(mine, mine, e_s, e_r, other)
    on_y(0, 1)
    on_y(3, 0)
    on_y(1, 0)
    on_y(1, 1)
    on_z(2)
    for d in (1, 3):
        on_x(d, 0, 0)
    on_y(4, 0)
    on_f(1)
    on_z(5)
    on_z(6)
    for d in (1, 3):
        on_x(d, 1, 0)
    ref = b_at(row, 1 - layer, 1 - layer)
    arrived(ref, e_s, e_r)
    to_x(ref, 1, 1)
    to_twin(ref, 3)
    on_y(2, 0)
    on_x(2, 0, 0)
    on_x(2, 1, 0)
    on_y(5, 0)
    for d in (1, 3, 2):
        on_x(d, 0, 1)
    on_y(6, 0)
    for d in (1, 3, 2):
        on_x(d, 1, 1)
    for n in (3, 4, 2, 5, 6):
        on_y(n, 1)
    for n in (0, 3, 4, 2, 5, 6):
        on_f(n)
    for m in range(4):
        on_far(m)
    for n in range(4):
        h, s = (layer, 1 - layer)[n // 2], (layer, 1 - layer)[n % 2]
        arrived(b_at(twin, h, s), t_s.at[n], t_r.at[n])
        for d in (1, 2, 3):
            there = ((x + XS - d) % XS) * 2 + 1 - core
            m = 4 + n * 3 + d - 1
            arrived(b_at(there, h, s), t_s.at[m], t_r.at[m])
    for copy in sends:
        copy.wait_send()
    for copy in local:
        copy.wait()


def gather(d, p):
    wide = jax.ShapeDtypeStruct((TILES, 2, UNIT, W), BF16)
    dma = pltpu.SemaphoreType.DMA
    return pl.pallas_call(
        gather_kernel,
        out_shape=(wide, wide),
        in_specs=[pl.BlockSpec(memory_space=pltpu.VMEM)] * 2,
        out_specs=(pl.BlockSpec(memory_space=pltpu.VMEM),) * 2,
        scratch_shapes=[
            dma, dma,
            dma((7,)), dma((7,)),
            dma((7, 2)), dma((7, 2)),
            dma((7,)), dma((7,)),
            dma((4,)), dma((4,)),
            dma((4, 3)), dma((4, 3)),
            dma((16,)), dma((16,)),
            dma((2,)),
        ],
        compiler_params=pltpu.CompilerParams(
            collective_id=0, has_side_effects=True, vmem_limit_bytes=30 << 20
        ),
        name="gather",
    )(d, p)


def multiply_kernel(a_ref, b_ref, o_ref, acc, codes, scalars, sem):
    col = lax.axis_index("col")
    sub = lax.broadcasted_iota(jnp.int32, (HALF, W), 0)
    place = lanes(HALF) % B

    def turn(v):
        return jnp.concatenate([v[:, B:], v[:, :B]], axis=1)

    def pattern(ref, t):
        one = ref[t, 0, pl.ds(BODY, PAIRS), :].astype(F32)
        two = ref[t, 1, pl.ds(BODY, PAIRS), :].astype(F32)
        left = lanes(PAIRS) < B
        return jnp.concatenate([jnp.where(left, one, turn(two)), jnp.where(left, turn(one), two)], axis=0)

    def in_row(block):
        return jnp.sum(jnp.where(place == sub, block, 0.0), axis=0, keepdims=True)

    want = in_row(pattern(a_ref, col))
    want_turned = turn(want)
    right = lanes(1) >= B
    used = lanes(1) % B < HALF
    for t in range(TILES):
        inner = in_row(pattern(a_ref, t))
        table = pattern(b_ref, t)
        hot = inner == sub.astype(F32)
        own = jnp.sum(jnp.where(hot, table, 0.0), axis=0, keepdims=True)
        other = jnp.sum(jnp.where(hot, turn(table), 0.0), axis=0, keepdims=True)
        live = used & (inner >= 0)

        def same(u, v):
            return jnp.where(live & (u == v) & (v >= 0), 1, 0)

        f0, f1 = same(own, want), same(other, want)
        f2, f3 = same(own, want_turned), same(other, want_turned)
        flags = (
            jnp.where(right, f3, f0) + 2 * jnp.where(right, f0, f3)
            + 4 * jnp.where(right, f2, f1) + 8 * jnp.where(right, f1, f2)
        )
        codes[pl.ds(t, 1), :] = jnp.where(flags > 0, flags + 16 * inner.astype(jnp.int32), 0)
    copy = pltpu.make_async_copy(codes, scalars, sem)
    copy.start()

    @pl.loop(0, HALF)
    def _(j):
        acc[j] = jnp.zeros((B, W), F32)

    copy.wait()
    left = lanes(1) < B

    @pl.loop(0, TILES)
    def _(t):
        for s in (0, 1):
            for q in (0, 1):
                @pl.loop(0, PAIRS, unroll=8)
                def _(j):
                    code = scalars[t, s * B + q * PAIRS + j]

                    @pl.when(code > 0)
                    def _():
                        k = code // 16
                        at = pl.ds(pl.multiple_of(k % PAIRS * B, B), B)
                        far = k // PAIRS

                        def pick(bit_left, bit_right):
                            return jnp.where(left, (code // bit_left) % 2, (code // bit_right) % 2).astype(F32)

                        def shifted(v, by):
                            return jnp.where(by == 1, turn(v), v)

                        one, two = b_ref[t, 0, at, :].astype(F32), b_ref[t, 1, at, :].astype(F32)
                        v = jnp.where(left, shifted(one, far), shifted(two, 1 - far))
                        w = (v * pick(1, 2) + turn(v) * pick(4, 8)).astype(BF16)
                        a = a_ref[t, s, pl.ds(pl.multiple_of(j * B, B), B), :]
                        acc[q * PAIRS + j] += jnp.dot(a[:, q * B:(q + 1) * B], w, preferred_element_type=F32)

    @pl.loop(0, PAIRS)
    def _(j):
        at = pl.ds(pl.multiple_of(j * B, B), B)
        one, two = a_ref[col, 0, at, :].astype(F32), a_ref[col, 1, at, :].astype(F32)
        for q in (0, 1):
            full = acc[q * PAIRS + j]
            mine = jnp.where(left, one, turn(two)) if q == 0 else jnp.where(left, turn(one), two)
            raised = 2.0 * mine - full
            o_ref[0, q * PAIRS + j] = jnp.where(left, full, turn(raised)).astype(BF16)
            o_ref[1, q * PAIRS + j] = jnp.where(left, turn(full), raised).astype(BF16)


def multiply(a, b):
    return pl.pallas_call(
        multiply_kernel,
        out_shape=jax.ShapeDtypeStruct((2, HALF, B, W), BF16),
        in_specs=[pl.BlockSpec(memory_space=pltpu.VMEM)] * 2,
        out_specs=pl.BlockSpec(memory_space=pltpu.VMEM),
        scratch_shapes=[
            pltpu.VMEM((HALF, B, W), F32),
            pltpu.VMEM((TILES, W), jnp.int32),
            pltpu.SMEM((TILES, W), jnp.int32),
            pltpu.SemaphoreType.DMA,
        ],
        compiler_params=pltpu.CompilerParams(vmem_limit_bytes=32 << 20),
        name="multiply",
    )(a, b)


CUTS = 4


def swap_kernel(o_ref, sq_ref, ra_ref, got, s_sem, r_sem):
    layer = lax.axis_index("layer")
    other = {"layer": 1 - layer}
    barrier = pltpu.get_barrier_semaphore()
    pl.semaphore_signal(barrier, inc=1, device_id=other, device_id_type=MESH)
    pl.semaphore_wait(barrier, 1)
    size = HALF // CUTS
    copies = []
    for n in range(CUTS):
        at = pl.ds(n * size, size)
        copy = pltpu.make_async_remote_copy(
            src_ref=o_ref.at[1 - layer, at], dst_ref=got.at[at], send_sem=s_sem.at[n], recv_sem=r_sem.at[n],
            device_id=other, device_id_type=MESH,
        )
        copy.start()
        copies.append(copy)

    @pl.loop(0, HALF)
    def _(j):
        both = o_ref[layer, j]
        sq_ref[layer * HALF + j] = both[:, :B]
        ra_ref[layer * HALF + j] = both[:, B:]

    for n, copy in enumerate(copies):
        copy.wait_recv()

        @pl.loop(n * size, (n + 1) * size)
        def _(j):
            both = got[j]
            sq_ref[(1 - layer) * HALF + j] = both[:, :B]
            ra_ref[(1 - layer) * HALF + j] = both[:, B:]

    for copy in copies:
        copy.wait_send()


def swap(o):
    out = jax.ShapeDtypeStruct((2 * HALF, B, B), BF16)
    return pl.pallas_call(
        swap_kernel,
        out_shape=(out, out),
        in_specs=[pl.BlockSpec(memory_space=pltpu.VMEM)],
        out_specs=(pl.BlockSpec(memory_space=pltpu.VMEM),) * 2,
        scratch_shapes=[
            pltpu.VMEM((HALF, B, W), BF16),
            pltpu.SemaphoreType.DMA((CUTS,)),
            pltpu.SemaphoreType.DMA((CUTS,)),
        ],
        compiler_params=pltpu.CompilerParams(
            collective_id=1, has_side_effects=True, vmem_limit_bytes=12 << 20
        ),
        name="swap",
    )(o)


def on_device(density, pattern):
    a, b = gather(density.reshape(2 * HALF, B, B), pattern.reshape(1, 2 * HALF))
    squared, raised = swap(multiply(a, b))
    return squared.reshape(density.shape), raised.reshape(density.shape)


def solution(mesh):
    placed = (P("row", "col", "layer", None, None), P("row", "col", "layer"))
    return jax.shard_map(
        on_device,
        mesh=mesh,
        in_specs=placed,
        out_specs=(P("row", "col", "layer", None, None), P("row", "col", "layer", None, None)),
        check_vma=False,
    )
```

time: 133 us -> 120 us (0.902)
  Pallas kernels: 129 us -> 115 us
    pallas_call x1, Pallas kernels: 98.8 us -> 75.7 us  [gather(): pl.pallas_call(gather_kernel, out_shape=(wide, wide), in_specs=[pl.BlockS...]
    pallas_call x1, Pallas kernels: 10 us -> 15.6 us  [swap(): pl.pallas_call(swap_kernel, out_shape=(out, out), in_specs=[pl.BlockSpec(...]
    pallas_call x1, Pallas kernels: 19.8 us -> 23.7 us  [multiply(): pl.pallas_call(multiply_kernel, out_shape=jax.ShapeDtypeStruct((2, HALF,...]
where the time goes in v2:
time: 120 us; the launch traced here: 119 us
  Pallas kernels  115 us (96%)
  local copies, waits for them, and re-layouts  3.81 us (3%)
    pallas_call x1, Pallas kernels, gather(): pl.pallas_call(gather_kernel, out_shape=(wide, wide), in_specs=[pl.BlockS...  75.7 us
    pallas_call x1, Pallas kernels, multiply(): pl.pallas_call(multiply_kernel, out_shape=jax.ShapeDtypeStruct((2, HALF,...  23.7 us
    pallas_call x1, Pallas kernels, swap(): pl.pallas_call(swap_kernel, out_shape=(out, out), in_specs=[pl.BlockSpec(...  15.6 us
    unnamed x6, local copies, waits for them, and re-layouts  3.81 us

profile of v2, /device:TPU:2, one launch (start us, length us, event | category | flops | bytes accessed | tf_op | source)
XLA Modules:
  0.0 119.5 jit_solution(15939588239491589468)
XLA Ops:
  0.6 0.0 copy-start
  0.6 1.2 %copy-done = bf16[64,1,1,64,64]{4,3,2,1,0:T(8,128)(2,1)S(1)} copy-done((bf16[64,1,1,64,64]{4,3,2,1,0:T(8,128)(2,1)S(1)}, bf16[64,1,1,64,64]{4,3,2,1,0:T(8,128)(2,1)}, u32[]{:S(2)}) %copy-start) | copy-done | bytes 524312
  1.9 0.0 copy-start.1
  1.9 0.7 copy-done.1
  2.5 75.7 %gather.1 = (bf16[16,2,1040,128]{3,2,1,0:T(8,128)(2,1)S(1)}, bf16[16,2,1040,128]{3,2,1,0:T(8,128)(2,1)S(1)}) custom-call(bf16[64,64,64]{2,1,0:T(8,128)(2,1)S(1)} %bitcast.8, s32[1,64]{1,0:T(1,128)S(1)} %bitcast.11), custom_call_target="tpu_custom_call" | custom-call | tf_op jit(solution)/shard_map/gather/pallas_call | solution.py:228
  78.2 23.7 %multiply.1.o_ref = bf16[2,32,64,128]{3,2,1,0:T(8,128)(2,1)S(1)} custom-call(bf16[16,2,1040,128]{3,2,1,0:T(8,128)(2,1)S(1)} %get-tuple-element.6.a_ref, bf16[16,2,1040,128]{3,2,1,0:T(8,128)(2,1)S(1)} %get-tuple-element.7.b_ref), custom_call_target="tpu_custom_call" | custom-call | tf_op jit(solution)/shard_map/multiply/pallas_call | solution.py:338
  101.9 15.6 %swap.1 = (bf16[64,64,64]{2,1,0:T(8,128)(2,1)S(1)}, bf16[64,64,64]{2,1,0:T(8,128)(2,1)S(1)}) custom-call(bf16[2,32,64,128]{3,2,1,0:T(8,128)(2,1)S(1)} %multiply.1.o_ref), custom_call_target="tpu_custom_call" | custom-call | tf_op jit(solution)/shard_map/swap/pallas_call | solution.py:395
  117.5 1.0 copy.8
  118.5 1.0 copy.9
Async XLA Ops:
  0.6 1.2 %copy-start = (bf16[64,1,1,64,64]{4,3,2,1,0:T(8,128)(2,1)S(1)}, bf16[64,1,1,64,64]{4,3,2,1,0:T(8,128)(2,1)}, u32[]{:S(2)}) copy-start(bf16[64,1,1,64,64]{4,3,2,1,0:T(8,128)(2,1)} %param.2) | copy-start | bytes 1572868
  1.9 0.7 copy-start.1

commit v3 on v2

--- a/solution.py
+++ b/solution.py
@@ -247,80 +247,123 @@
     )(d, p)
 
 
-def multiply_kernel(a_ref, b_ref, o_ref, acc, codes, scalars, sem):
-    col = lax.axis_index("col")
+CHUNK = W
+MOST = TILES * 2 * HALF
+
+
+def turn(v):
+    return jnp.concatenate([v[:, B:], v[:, :B]], axis=1)
+
+
+def pattern(ref, t):
+    one = ref[t, 0, pl.ds(BODY, PAIRS), :].astype(F32)
+    two = ref[t, 1, pl.ds(BODY, PAIRS), :].astype(F32)
+    near = lanes(PAIRS) < B
+    return jnp.concatenate([jnp.where(near, one, turn(two)), jnp.where(near, turn(one), two)], axis=0)
+
+
+def in_row(block):
     sub = lax.broadcasted_iota(jnp.int32, (HALF, W), 0)
-    place = lanes(HALF) % B
-
-    def turn(v):
-        return jnp.concatenate([v[:, B:], v[:, :B]], axis=1)
-
-    def pattern(ref, t):
-        one = ref[t, 0, pl.ds(BODY, PAIRS), :].astype(F32)
-        two = ref[t, 1, pl.ds(BODY, PAIRS), :].astype(F32)
-        left = lanes(PAIRS) < B
-        return jnp.concatenate([jnp.where(left, one, turn(two)), jnp.where(left, turn(one), two)], axis=0)
-
-    def in_row(block):
-        return jnp.sum(jnp.where(place == sub, block, 0.0), axis=0, keepdims=True)
-
-    want = in_row(pattern(a_ref, col))
+    return jnp.sum(jnp.where(lanes(HALF) % B == sub, block, 0.0), axis=0, keepdims=True)
+
+
+def match(a_ref, b_ref, codes, t, want):
     want_turned = turn(want)
     right = lanes(1) >= B
     used = lanes(1) % B < HALF
+    inner = in_row(pattern(a_ref, t))
+    table = pattern(b_ref, t)
+    hot = inner == lax.broadcasted_iota(jnp.int32, (HALF, W), 0).astype(F32)
+    own = jnp.sum(jnp.where(hot, table, 0.0), axis=0, keepdims=True)
+    other = jnp.sum(jnp.where(hot, turn(table), 0.0), axis=0, keepdims=True)
+    live = used & (inner >= 0)
+
+    def same(u, v):
+        return jnp.where(live & (u == v) & (v >= 0), 1, 0)
+
+    f0, f1 = same(own, want), same(other, want)
+    f2, f3 = same(own, want_turned), same(other, want_turned)
+    flags = (
+        jnp.where(right, f3, f0) + 2 * jnp.where(right, f0, f3)
+        + 4 * jnp.where(right, f2, f1) + 8 * jnp.where(right, f1, f2)
+    )
+    place = lanes(1) % B + jnp.where(right, HALF, 0) + t * 2 * HALF
+    codes[pl.ds(t, 1), :] = jnp.where(flags > 0, flags + 16 * inner.astype(jnp.int32) + 512 * place, 0)
+
+
+def multiply_kernel(a_ref, b_ref, o_ref, acc, codes, ranks, hits, listed, total, counts, sem):
+    col = lax.axis_index("col")
+    want = in_row(pattern(a_ref, col))
     for t in range(TILES):
-        inner = in_row(pattern(a_ref, t))
-        table = pattern(b_ref, t)
-        hot = inner == sub.astype(F32)
-        own = jnp.sum(jnp.where(hot, table, 0.0), axis=0, keepdims=True)
-        other = jnp.sum(jnp.where(hot, turn(table), 0.0), axis=0, keepdims=True)
-        live = used & (inner >= 0)
-
-        def same(u, v):
-            return jnp.where(live & (u == v) & (v >= 0), 1, 0)
-
-        f0, f1 = same(own, want), same(other, want)
-        f2, f3 = same(own, want_turned), same(other, want_turned)
-        flags = (
-            jnp.where(right, f3, f0) + 2 * jnp.where(right, f0, f3)
-            + 4 * jnp.where(right, f2, f1) + 8 * jnp.where(right, f1, f2)
-        )
-        codes[pl.ds(t, 1), :] = jnp.where(flags > 0, flags + 16 * inner.astype(jnp.int32), 0)
-    copy = pltpu.make_async_copy(codes, scalars, sem)
-    copy.start()
+        match(a_ref, b_ref, codes, t, want)
+
+    code = codes[...]
+    hit = jnp.where(code > 0, 1.0, 0.0).astype(BF16)
+    down = lax.broadcasted_iota(jnp.int32, (W, W), 0)
+    before = jnp.where(down < lanes(W), 1.0, 0.0).astype(BF16)
+    in_tile = jnp.dot(hit, before, preferred_element_type=F32)
+    of_tile = jnp.dot(hit, jnp.ones((W, W), BF16), preferred_element_type=F32)
+    tiles = lax.broadcasted_iota(jnp.int32, (TILES, TILES), 0)
+    above = jnp.where(lax.broadcasted_iota(jnp.int32, (TILES, TILES), 1) < tiles, 1.0, 0.0).astype(BF16)
+    rank = in_tile + jnp.dot(above, of_tile.astype(BF16), preferred_element_type=F32)
+    ranks[...] = jnp.where(code > 0, rank, -1.0)
+    total[...] = jnp.broadcast_to(jnp.sum(of_tile, axis=0, keepdims=True).astype(jnp.int32), (8, W))
+    count = pltpu.make_async_copy(total, counts, sem)
+    count.start()
 
     @pl.loop(0, HALF)
     def _(j):
         acc[j] = jnp.zeros((B, W), F32)
 
-    copy.wait()
+    count.wait()
+    number = counts[0, 0]
+
+    @pl.loop(0, MOST // CHUNK)
+    def _(c):
+        @pl.when(c * CHUNK < number)
+        def _():
+            wanted = (down + c * CHUNK).astype(F32)
+            found = jnp.zeros((CHUNK, W), F32)
+            for t in range(TILES):
+                value = codes[pl.ds(t, 1), :].astype(F32)
+                found += jnp.where(ranks[pl.ds(t, 1), :] == wanted, value, 0.0)
+            column = jnp.sum(found, axis=1, keepdims=True)
+            line = jnp.sum(jnp.where(down == lanes(W), column, 0.0), axis=0, keepdims=True)
+            hits[...] = jnp.broadcast_to(line.astype(jnp.int32), (8, W))
+            copy = pltpu.make_async_copy(hits, listed, sem)
+            copy.start()
+            copy.wait()
+
+            @pl.loop(0, (jnp.minimum(number - c * CHUNK, CHUNK) + 3) // 4)
+            def _(n):
+                products = []
+                for m in range(4):
+                    code = listed[0, n * 4 + m]
+                    k, place = (code // 16) % HALF, code // 512
+                    t, s, j = place // (2 * HALF), (place // HALF) % 2, place % HALF
+                    at = pl.ds(pl.multiple_of(k % PAIRS * B, B), B)
+                    from_row = pl.ds(pl.multiple_of(j % PAIRS * B, B), B)
+                    far, q = k // PAIRS, j // PAIRS
+                    near = lanes(1) < B
+
+                    def pick(bit_left, bit_right):
+                        return jnp.where(near, (code // bit_left) % 2, (code // bit_right) % 2).astype(F32)
+
+                    one, two = b_ref[t, 0, at, :].astype(F32), b_ref[t, 1, at, :].astype(F32)
+                    v = jnp.where(
+                        far == 1,
+                        jnp.where(near, turn(one), two),
+                        jnp.where(near, one, turn(two)),
+                    )
+                    w = (v * pick(1, 2) + turn(v) * pick(4, 8)).astype(BF16)
+                    a = a_ref[t, s, from_row, :]
+                    a = a * jnp.where(lanes(1) // B == q, 1.0, 0.0).astype(BF16)
+                    both = jnp.concatenate([w, w], axis=0)
+                    products.append((j, jnp.dot(a, both, preferred_element_type=F32)))
+                for j, product in products:
+                    acc[j] += product
+
     left = lanes(1) < B
-
-    @pl.loop(0, TILES)
-    def _(t):
-        for s in (0, 1):
-            for q in (0, 1):
-                @pl.loop(0, PAIRS, unroll=8)
-                def _(j):
-                    code = scalars[t, s * B + q * PAIRS + j]
-
-                    @pl.when(code > 0)
-                    def _():
-                        k = code // 16
-                        at = pl.ds(pl.multiple_of(k % PAIRS * B, B), B)
-                        far = k // PAIRS
-
-                        def pick(bit_left, bit_right):
-                            return jnp.where(left, (code // bit_left) % 2, (code // bit_right) % 2).astype(F32)
-
-                        def shifted(v, by):
-                            return jnp.where(by == 1, turn(v), v)
-
-                        one, two = b_ref[t, 0, at, :].astype(F32), b_ref[t, 1, at, :].astype(F32)
-                        v = jnp.where(left, shifted(one, far), shifted(two, 1 - far))
-                        w = (v * pick(1, 2) + turn(v) * pick(4, 8)).astype(BF16)
-                        a = a_ref[t, s, pl.ds(pl.multiple_of(j * B, B), B), :]
-                        acc[q * PAIRS + j] += jnp.dot(a[:, q * B:(q + 1) * B], w, preferred_element_type=F32)
 
     @pl.loop(0, PAIRS)
     def _(j):
@@ -343,7 +386,11 @@
         scratch_shapes=[
             pltpu.VMEM((HALF, B, W), F32),
             pltpu.VMEM((TILES, W), jnp.int32),
-            pltpu.SMEM((TILES, W), jnp.int32),
+            pltpu.VMEM((TILES, W), F32),
+            pltpu.VMEM((8, W), jnp.int32),
+            pltpu.SMEM((8, W), jnp.int32),
+            pltpu.VMEM((8, W), jnp.int32),
+            pltpu.SMEM((8, W), jnp.int32),
             pltpu.SemaphoreType.DMA,
         ],
         compiler_params=pltpu.CompilerParams(vmem_limit_bytes=32 << 20),

time: 120 us -> 103 us (0.86)
  Pallas kernels: 115 us -> 97.6 us
    pallas_call x1, Pallas kernels: 23.7 us -> 6.85 us  [multiply(): pl.pallas_call(multiply_kernel, out_shape=jax.ShapeDtypeStruct((2, HALF,...]
where the time goes in v3:
time: 103 us; the launch traced here: 102 us
  Pallas kernels  97.6 us (95%)
  local copies, waits for them, and re-layouts  3.81 us (4%)
    pallas_call x1, Pallas kernels, gather(): pl.pallas_call(gather_kernel, out_shape=(wide, wide), in_specs=[pl.BlockS...  75.7 us
    pallas_call x1, Pallas kernels, swap(): pl.pallas_call(swap_kernel, out_shape=(out, out), in_specs=[pl.BlockSpec(...  15.1 us
    pallas_call x1, Pallas kernels, multiply(): pl.pallas_call(multiply_kernel, out_shape=jax.ShapeDtypeStruct((2, HALF,...  6.85 us
    unnamed x6, local copies, waits for them, and re-layouts  3.81 us

profile of v3, /device:TPU:2, one launch (start us, length us, event | category | flops | bytes accessed | tf_op | source)
XLA Modules:
  0.0 102.1 jit_solution(14326276141128600806)
XLA Ops:
  0.6 0.0 copy-start
  0.6 1.2 %copy-done = bf16[64,1,1,64,64]{4,3,2,1,0:T(8,128)(2,1)S(1)} copy-done((bf16[64,1,1,64,64]{4,3,2,1,0:T(8,128)(2,1)S(1)}, bf16[64,1,1,64,64]{4,3,2,1,0:T(8,128)(2,1)}, u32[]{:S(2)}) %copy-start) | copy-done | bytes 524312
  1.9 0.0 copy-start.1
  1.9 0.7 copy-done.1
  2.5 75.7 %gather.1 = (bf16[16,2,1040,128]{3,2,1,0:T(8,128)(2,1)S(1)}, bf16[16,2,1040,128]{3,2,1,0:T(8,128)(2,1)S(1)}) custom-call(bf16[64,64,64]{2,1,0:T(8,128)(2,1)S(1)} %bitcast.8, s32[1,64]{1,0:T(1,128)S(1)} %bitcast.11), custom_call_target="tpu_custom_call" | custom-call | tf_op jit(solution)/shard_map/gather/pallas_call | solution.py:228
  78.2 6.8 %multiply.1.o_ref = bf16[2,32,64,128]{3,2,1,0:T(8,128)(2,1)S(1)} custom-call(bf16[16,2,1040,128]{3,2,1,0:T(8,128)(2,1)S(1)} %get-tuple-element.6.a_ref, bf16[16,2,1040,128]{3,2,1,0:T(8,128)(2,1)S(1)} %get-tuple-element.7.b_ref), custom_call_target="tpu_custom_call" | custom-call | tf_op jit(solution)/shard_map/multiply/pallas_call | solution.py:381
  85.1 15.1 %swap.1 = (bf16[64,64,64]{2,1,0:T(8,128)(2,1)S(1)}, bf16[64,64,64]{2,1,0:T(8,128)(2,1)S(1)}) custom-call(bf16[2,32,64,128]{3,2,1,0:T(8,128)(2,1)S(1)} %multiply.1.o_ref), custom_call_target="tpu_custom_call" | custom-call | tf_op jit(solution)/shard_map/swap/pallas_call | solution.py:442
  100.2 1.0 copy.8
  101.1 1.0 copy.9
Async XLA Ops:
  0.6 1.2 %copy-start = (bf16[64,1,1,64,64]{4,3,2,1,0:T(8,128)(2,1)S(1)}, bf16[64,1,1,64,64]{4,3,2,1,0:T(8,128)(2,1)}, u32[]{:S(2)}) copy-start(bf16[64,1,1,64,64]{4,3,2,1,0:T(8,128)(2,1)} %param.2) | copy-start | bytes 1572868
  1.9 0.7 copy-start.1

commit v4 on v3

--- a/solution.py
+++ b/solution.py
@@ -291,7 +291,10 @@
     codes[pl.ds(t, 1), :] = jnp.where(flags > 0, flags + 16 * inner.astype(jnp.int32) + 512 * place, 0)
 
 
-def multiply_kernel(a_ref, b_ref, o_ref, acc, codes, ranks, hits, listed, total, counts, sem):
+GROUP = 8
+
+
+def multiply_kernel(a_ref, b_ref, acc, codes, ranks, hits, listed, sem):
     col = lax.axis_index("col")
     want = in_row(pattern(a_ref, col))
     for t in range(TILES):
@@ -307,88 +310,74 @@
     above = jnp.where(lax.broadcasted_iota(jnp.int32, (TILES, TILES), 1) < tiles, 1.0, 0.0).astype(BF16)
     rank = in_tile + jnp.dot(above, of_tile.astype(BF16), preferred_element_type=F32)
     ranks[...] = jnp.where(code > 0, rank, -1.0)
-    total[...] = jnp.broadcast_to(jnp.sum(of_tile, axis=0, keepdims=True).astype(jnp.int32), (8, W))
-    count = pltpu.make_async_copy(total, counts, sem)
-    count.start()
+    total = jnp.sum(of_tile, axis=0, keepdims=True).astype(jnp.int32)
+    hits[...] = jnp.broadcast_to(total, (8, W))
+
+    def enlist(c):
+        wanted = (down + c * CHUNK).astype(F32)
+        found = jnp.zeros((CHUNK, W), F32)
+        for t in range(TILES):
+            found += jnp.where(ranks[pl.ds(t, 1), :] == wanted, codes[pl.ds(t, 1), :].astype(F32), 0.0)
+        column = jnp.sum(found, axis=1, keepdims=True)
+        line = jnp.sum(jnp.where(down == lanes(W), column, 0.0), axis=0, keepdims=True)
+        hits[pl.ds(0, 1), :] = line.astype(jnp.int32)
+        copy = pltpu.make_async_copy(hits, listed, sem)
+        copy.start()
+        return copy
+
+    def product(code):
+        k, place = (code // 16) % HALF, code // 512
+        t, s, j = place // (2 * HALF), (place // HALF) % 2, place % HALF
+        at = pl.ds(pl.multiple_of(k % PAIRS * B, B), B)
+        from_row = pl.ds(pl.multiple_of(j % PAIRS * B, B), B)
+        far, q = k // PAIRS, j // PAIRS
+        near = lanes(1) < B
+
+        def pick(bit_left, bit_right):
+            return jnp.where(near, (code // bit_left) % 2, (code // bit_right) % 2).astype(F32)
+
+        stay = b_ref[t, far, at, :].astype(F32)
+        move = b_ref[t, 1 - far, at, :].astype(F32)
+        here = lanes(B) // B == far
+        straight = jnp.where(here, stay, turn(move))
+        crossed = jnp.where(here, move, turn(stay))
+        w = (straight * pick(1, 2) + crossed * pick(4, 8)).astype(BF16)
+        a = a_ref[t, s, from_row, :] * jnp.where(lanes(1) // B == q, 1.0, 0.0).astype(BF16)
+        return j, jnp.dot(a, jnp.concatenate([w, w], axis=0), preferred_element_type=F32)
+
+    def run(number):
+        @pl.loop(0, (number + GROUP - 1) // GROUP)
+        def _(n):
+            for j, value in [product(listed[0, n * GROUP + m]) for m in range(GROUP)]:
+                acc[j] += value
+
+    first = enlist(0)
 
     @pl.loop(0, HALF)
     def _(j):
         acc[j] = jnp.zeros((B, W), F32)
 
-    count.wait()
-    number = counts[0, 0]
-
-    @pl.loop(0, MOST // CHUNK)
+    first.wait()
+    number = listed[1, 0]
+    run(jnp.minimum(number, CHUNK))
+
+    @pl.loop(1, MOST // CHUNK)
     def _(c):
         @pl.when(c * CHUNK < number)
         def _():
-            wanted = (down + c * CHUNK).astype(F32)
-            found = jnp.zeros((CHUNK, W), F32)
-            for t in range(TILES):
-                value = codes[pl.ds(t, 1), :].astype(F32)
-                found += jnp.where(ranks[pl.ds(t, 1), :] == wanted, value, 0.0)
-            column = jnp.sum(found, axis=1, keepdims=True)
-            line = jnp.sum(jnp.where(down == lanes(W), column, 0.0), axis=0, keepdims=True)
-            hits[...] = jnp.broadcast_to(line.astype(jnp.int32), (8, W))
-            copy = pltpu.make_async_copy(hits, listed, sem)
-            copy.start()
-            copy.wait()
-
-            @pl.loop(0, (jnp.minimum(number - c * CHUNK, CHUNK) + 3) // 4)
-            def _(n):
-                products = []
-                for m in range(4):
-                    code = listed[0, n * 4 + m]
-                    k, place = (code // 16) % HALF, code // 512
-                    t, s, j = place // (2 * HALF), (place // HALF) % 2, place % HALF
-                    at = pl.ds(pl.multiple_of(k % PAIRS * B, B), B)
-                    from_row = pl.ds(pl.multiple_of(j % PAIRS * B, B), B)
-                    far, q = k // PAIRS, j // PAIRS
-                    near = lanes(1) < B
-
-                    def pick(bit_left, bit_right):
-                        return jnp.where(near, (code // bit_left) % 2, (code // bit_right) % 2).astype(F32)
-
-                    one, two = b_ref[t, 0, at, :].astype(F32), b_ref[t, 1, at, :].astype(F32)
-                    v = jnp.where(
-                        far == 1,
-                        jnp.where(near, turn(one), two),
-                        jnp.where(near, one, turn(two)),
-                    )
-                    w = (v * pick(1, 2) + turn(v) * pick(4, 8)).astype(BF16)
-                    a = a_ref[t, s, from_row, :]
-                    a = a * jnp.where(lanes(1) // B == q, 1.0, 0.0).astype(BF16)
-                    both = jnp.concatenate([w, w], axis=0)
-                    products.append((j, jnp.dot(a, both, preferred_element_type=F32)))
-                for j, product in products:
-                    acc[j] += product
-
-    left = lanes(1) < B
-
-    @pl.loop(0, PAIRS)
-    def _(j):
-        at = pl.ds(pl.multiple_of(j * B, B), B)
-        one, two = a_ref[col, 0, at, :].astype(F32), a_ref[col, 1, at, :].astype(F32)
-        for q in (0, 1):
-            full = acc[q * PAIRS + j]
-            mine = jnp.where(left, one, turn(two)) if q == 0 else jnp.where(left, turn(one), two)
-            raised = 2.0 * mine - full
-            o_ref[0, q * PAIRS + j] = jnp.where(left, full, turn(raised)).astype(BF16)
-            o_ref[1, q * PAIRS + j] = jnp.where(left, turn(full), raised).astype(BF16)
+            enlist(c).wait()
+            run(jnp.minimum(number - c * CHUNK, CHUNK))
 
 
 def multiply(a, b):
     return pl.pallas_call(
         multiply_kernel,
-        out_shape=jax.ShapeDtypeStruct((2, HALF, B, W), BF16),
+        out_shape=jax.ShapeDtypeStruct((HALF, B, W), F32),
         in_specs=[pl.BlockSpec(memory_space=pltpu.VMEM)] * 2,
         out_specs=pl.BlockSpec(memory_space=pltpu.VMEM),
         scratch_shapes=[
-            pltpu.VMEM((HALF, B, W), F32),
             pltpu.VMEM((TILES, W), jnp.int32),
             pltpu.VMEM((TILES, W), F32),
-            pltpu.VMEM((8, W), jnp.int32),
-            pltpu.SMEM((8, W), jnp.int32),
             pltpu.VMEM((8, W), jnp.int32),
             pltpu.SMEM((8, W), jnp.int32),
             pltpu.SemaphoreType.DMA,
@@ -401,64 +390,78 @@
 CUTS = 4
 
 
-def swap_kernel(o_ref, sq_ref, ra_ref, got, s_sem, r_sem):
-    layer = lax.axis_index("layer")
+def swap_kernel(acc, a_ref, sq_ref, ra_ref, out, got, s_sem, r_sem):
+    layer, col = lax.axis_index("layer"), lax.axis_index("col")
     other = {"layer": 1 - layer}
     barrier = pltpu.get_barrier_semaphore()
     pl.semaphore_signal(barrier, inc=1, device_id=other, device_id_type=MESH)
-    pl.semaphore_wait(barrier, 1)
     size = HALF // CUTS
+    near = lanes(1) < B
+
+    def finish(n):
+        @pl.loop(n * size // 2, (n + 1) * size // 2)
+        def _(j):
+            at = pl.ds(pl.multiple_of(j * B, B), B)
+            one, two = a_ref[col, 0, at, :].astype(F32), a_ref[col, 1, at, :].astype(F32)
+            for q in (0, 1):
+                full = acc[q * PAIRS + j]
+                mine = jnp.where(near, one, turn(two)) if q == 0 else jnp.where(near, turn(one), two)
+                raised = 2.0 * mine - full
+                out[0, 2 * j + q] = jnp.where(near, full, turn(raised)).astype(BF16)
+                out[1, 2 * j + q] = jnp.where(near, turn(full), raised).astype(BF16)
+
+    def unpack(both, half, n):
+        @pl.loop(n * size // 2, (n + 1) * size // 2)
+        def _(j):
+            for q in (0, 1):
+                v = both[2 * j + q]
+                sq_ref[half * HALF + q * PAIRS + j] = v[:, :B]
+                ra_ref[half * HALF + q * PAIRS + j] = v[:, B:]
+
     copies = []
     for n in range(CUTS):
+        finish(n)
+        if n == 0:
+            pl.semaphore_wait(barrier, 1)
         at = pl.ds(n * size, size)
         copy = pltpu.make_async_remote_copy(
-            src_ref=o_ref.at[1 - layer, at], dst_ref=got.at[at], send_sem=s_sem.at[n], recv_sem=r_sem.at[n],
+            src_ref=out.at[1 - layer, at], dst_ref=got.at[at], send_sem=s_sem.at[n], recv_sem=r_sem.at[n],
             device_id=other, device_id_type=MESH,
         )
         copy.start()
         copies.append(copy)
-
-    @pl.loop(0, HALF)
-    def _(j):
-        both = o_ref[layer, j]
-        sq_ref[layer * HALF + j] = both[:, :B]
-        ra_ref[layer * HALF + j] = both[:, B:]
-
+    for n in range(CUTS):
+        unpack(out.at[layer], layer, n)
     for n, copy in enumerate(copies):
         copy.wait_recv()
-
-        @pl.loop(n * size, (n + 1) * size)
-        def _(j):
-            both = got[j]
-            sq_ref[(1 - layer) * HALF + j] = both[:, :B]
-            ra_ref[(1 - layer) * HALF + j] = both[:, B:]
-
+        unpack(got, 1 - layer, n)
     for copy in copies:
         copy.wait_send()
 
 
-def swap(o):
+def swap(acc, a):
     out = jax.ShapeDtypeStruct((2 * HALF, B, B), BF16)
     return pl.pallas_call(
         swap_kernel,
         out_shape=(out, out),
-        in_specs=[pl.BlockSpec(memory_space=pltpu.VMEM)],
+        in_specs=[pl.BlockSpec(memory_space=pltpu.VMEM)] * 2,
         out_specs=(pl.BlockSpec(memory_space=pltpu.VMEM),) * 2,
         scratch_shapes=[
+            pltpu.VMEM((2, HALF, B, W), BF16),
             pltpu.VMEM((HALF, B, W), BF16),
             pltpu.SemaphoreType.DMA((CUTS,)),
             pltpu.SemaphoreType.DMA((CUTS,)),
         ],
         compiler_params=pltpu.CompilerParams(
-            collective_id=1, has_side_effects=True, vmem_limit_bytes=12 << 20
+            collective_id=1, has_side_effects=True, vmem_limit_bytes=24 << 20
         ),
         name="swap",
-    )(o)
+    )(acc, a)
 
 
 def on_device(density, pattern):
     a, b = gather(density.reshape(2 * HALF, B, B), pattern.reshape(1, 2 * HALF))
-    squared, raised = swap(multiply(a, b))
+    squared, raised = swap(multiply(a, b), a)
     return squared.reshape(density.shape), raised.reshape(density.shape)
 
 

time: 103 us -> 100 us (0.971)
  the two profiles are of different devices: /device:TPU:2 before, /device:TPU:5 now
where the time goes in v4:
time: 100 us
  Pallas kernels  95.7 us (96%)
  local copies, waits for them, and re-layouts  3.81 us (4%)
    pallas_call x1, Pallas kernels, gather(): pl.pallas_call(gather_kernel, out_shape=(wide, wide), in_specs=[pl.BlockS...  72.4 us
    pallas_call x1, Pallas kernels, swap(): pl.pallas_call(swap_kernel, out_shape=(out, out), in_specs=[pl.BlockSpec(...  18.7 us
    pallas_call x1, Pallas kernels, multiply(): pl.pallas_call(multiply_kernel, out_shape=jax.ShapeDtypeStruct((HALF, B,...  4.59 us
    unnamed x6, local copies, waits for them, and re-layouts  3.81 us

profile of v4, /device:TPU:5, one launch (start us, length us, event | category | flops | bytes accessed | tf_op | source)
XLA Modules:
  0.0 100.2 jit_solution(4381115755574544723)
XLA Ops:
  0.6 0.0 copy-start
  0.6 1.2 %copy-done = bf16[64,1,1,64,64]{4,3,2,1,0:T(8,128)(2,1)S(1)} copy-done((bf16[64,1,1,64,64]{4,3,2,1,0:T(8,128)(2,1)S(1)}, bf16[64,1,1,64,64]{4,3,2,1,0:T(8,128)(2,1)}, u32[]{:S(2)}) %copy-start) | copy-done | bytes 524312
  1.9 0.0 copy-start.1
  1.9 0.7 copy-done.1
  2.5 72.4 %gather.1 = (bf16[16,2,1040,128]{3,2,1,0:T(8,128)(2,1)S(1)}, bf16[16,2,1040,128]{3,2,1,0:T(8,128)(2,1)S(1)}) custom-call(bf16[64,64,64]{2,1,0:T(8,128)(2,1)S(1)} %bitcast.8, s32[1,64]{1,0:T(1,128)S(1)} %bitcast.11), custom_call_target="tpu_custom_call" | custom-call | tf_op jit(solution)/shard_map/gather/pallas_call | solution.py:228
  75.0 4.6 %multiply.1.acc = f32[32,64,128]{2,1,0:T(8,128)S(1)} custom-call(bf16[16,2,1040,128]{3,2,1,0:T(8,128)(2,1)S(1)} %get-tuple-element.6.a_ref, bf16[16,2,1040,128]{3,2,1,0:T(8,128)(2,1)S(1)} %get-tuple-element.7.b_ref), custom_call_target="tpu_custom_call" | custom-call | tf_op jit(solution)/shard_map/multiply/pallas_call | solution.py:373
  79.6 18.7 %swap.1 = (bf16[64,64,64]{2,1,0:T(8,128)(2,1)S(1)}, bf16[64,64,64]{2,1,0:T(8,128)(2,1)S(1)}) custom-call(f32[32,64,128]{2,1,0:T(8,128)S(1)} %multiply.1.acc, bf16[16,2,1040,128]{3,2,1,0:T(8,128)(2,1)S(1)} %get-tuple-element.6.a_ref), custom_call_target="tpu_custom_call" | custom-call | tf_op jit(solution)/shard_map/swap/pallas_call | solution.py:444
  98.2 1.0 copy.8
  99.2 1.0 copy.9
Async XLA Ops:
  0.6 1.2 %copy-start = (bf16[64,1,1,64,64]{4,3,2,1,0:T(8,128)(2,1)S(1)}, bf16[64,1,1,64,64]{4,3,2,1,0:T(8,128)(2,1)}, u32[]{:S(2)}) copy-start(bf16[64,1,1,64,64]{4,3,2,1,0:T(8,128)(2,1)} %param.2) | copy-start | bytes 1572868
  1.9 0.7 copy-start.1

commit v5 on v4

--- a/solution.py
+++ b/solution.py
@@ -16,6 +16,8 @@
 BODY = PAIRS * B
 UNIT = BODY + PAIRS
 TILES = 16
+CUT = (0, 528, 1040)
+PIECES = range(len(CUT) - 1)
 YS, ZS, XS = 4, 4, 4
 
 
@@ -98,9 +100,12 @@
     def sense(n):
         return 1 + 2 * ((n + core) % 2)
 
-    def to_y(src, n):
+    def piece(ref, p):
+        return ref.at[pl.ds(CUT[p], CUT[p + 1] - CUT[p])]
+
+    def to_y(src, n, p):
         for k, d in enumerate((sense(n), 4 - sense(n))):
-            send(src, a_at(0, n), y_s.at[n, k], y_r.at[n, k], {"col": at_y(d)})
+            send(piece(src, p), piece(a_at(0, n), p), y_s.at[n, k, p], y_r.at[n, k, p], {"col": at_y(d)})
 
     def to_x(src, h, own):
         n = h * 2 + own
@@ -115,55 +120,52 @@
         copy.start()
         local.append(copy)
 
-    def pass_far(ref, m):
-        send(ref, ref, g_s.at[m], g_r.at[m], {"col": at_z(step)})
-
-    to_y(mine, 0)
-    send(theirs, theirs, z_s.at[3], z_r.at[3], other)
-    send(mine, a_at(0, 0), z_s.at[1], z_r.at[1], {"col": at_z(step)})
-    send(theirs, a_at(0, 0), z_s.at[4], z_r.at[4], aside)
-    send(mine, a_at(0, 0), z_s.at[2], z_r.at[2], {"col": at_z(4 - step)})
+    def to_z(src, dst, n, p, peer):
+        send(piece(src, p), piece(dst, p), z_s.at[n, p], z_r.at[n, p], peer)
+
+    def pass_far(ref, m, p):
+        send(piece(ref, p), piece(ref, p), g_s.at[m, p], g_r.at[m, p], {"col": at_z(step)})
+
+    for p in PIECES:
+        to_y(mine, 0, p)
+        to_z(theirs, theirs, 3, p, other)
+        to_z(mine, a_at(0, 0), 1, p, {"col": at_z(step)})
+        to_z(theirs, a_at(0, 0), 4, p, aside)
+        to_z(mine, a_at(0, 0), 2, p, {"col": at_z(4 - step)})
     to_x(mine, 0, 0)
     to_x(theirs, 1, 0)
     to_twin(mine, 0)
     to_twin(theirs, 2)
     keep(mine, 0)
 
-    def on_z(n):
+    def on_z(n, p):
+        ref = b_at(row, layer, 1 - layer) if n == 3 else a_at(0, n)
+        arrived(piece(ref, p), z_s.at[n, p], z_r.at[n, p])
         if n == 3:
-            ref = b_at(row, layer, 1 - layer)
-            arrived(ref, z_s.at[n], z_r.at[n])
-            send(ref, a_at(0, 3), z_s.at[5], z_r.at[5], {"col": at_z(away)})
-        else:
-            ref = a_at(0, n)
-            arrived(ref, z_s.at[n], z_r.at[n])
-            if n == 1:
-                pass_far(ref, 0)
-            if n == 4:
-                send(ref, ref, z_s.at[6], z_r.at[6], {"col": at_z(4 - away)})
-        to_y(ref, n)
-        if n == 3:
-            to_x(ref, 0, 1)
-            to_twin(ref, 1)
-            keep(ref, 3)
-
-    def on_y(n, k):
+            to_z(ref, a_at(0, 3), 5, p, {"col": at_z(away)})
+        if n == 1:
+            pass_far(ref, 0, p)
+        if n == 4:
+            to_z(ref, ref, 6, p, {"col": at_z(4 - away)})
+        to_y(ref, n, p)
+
+    def on_y(n, k, p):
         d = (4 - sense(n), sense(n))[k]
         ref = a_at(d, n)
-        arrived(ref, y_s.at[n, k], y_r.at[n, k])
+        arrived(piece(ref, p), y_s.at[n, k, p], y_r.at[n, k, p])
         if n == 1:
-            pass_far(ref, 1 + k)
+            pass_far(ref, 1 + k, p)
         if k == 0:
-            send(ref, ref, f_s.at[n], f_r.at[n], {"col": at_y(sense(n))})
-
-    def on_f(n):
+            send(piece(ref, p), piece(ref, p), f_s.at[n, p], f_r.at[n, p], {"col": at_y(sense(n))})
+
+    def on_f(n, p):
         ref = a_at(2, n)
-        arrived(ref, f_s.at[n], f_r.at[n])
+        arrived(piece(ref, p), f_s.at[n, p], f_r.at[n, p])
         if n == 1:
-            pass_far(ref, 3)
-
-    def on_far(m):
-        arrived(a_at((0, 4 - sense(1), sense(1), 2)[m], 7), g_s.at[m], g_r.at[m])
+            pass_far(ref, 3, p)
+
+    def on_far(m, p):
+        arrived(piece(a_at((0, 4 - sense(1), sense(1), 2)[m], 7), p), g_s.at[m, p], g_r.at[m, p])
 
     def on_x(d, h, own):
         there = ((x + XS - d) % XS) * 2 + core
@@ -172,43 +174,53 @@
         arrived(ref, x_s.at[n, d - 1], x_r.at[n, d - 1])
         to_twin(ref, 4 + n * 3 + d - 1)
 
-    on_z(3)
-    on_z(1)
-    on_y(0, 0)
-    on_z(4)
-    send(mine, mine, e_s, e_r, other)
-    on_y(0, 1)
-    on_y(3, 0)
-    on_y(1, 0)
-    on_y(1, 1)
-    on_z(2)
+    for p in PIECES:
+        on_z(3, p)
+        if p == PIECES[-1]:
+            send(mine, mine, e_s, e_r, other)
+        on_z(1, p)
+        on_y(0, 0, p)
+        on_z(4, p)
+    ref = b_at(row, layer, 1 - layer)
+    to_x(ref, 0, 1)
+    to_twin(ref, 1)
+    keep(ref, 3)
+    for p in PIECES:
+        on_y(3, 0, p)
+        on_y(1, 0, p)
+        on_y(1, 1, p)
+        on_z(2, p)
     for d in (1, 3):
         on_x(d, 0, 0)
-    on_y(4, 0)
-    on_f(1)
-    on_z(5)
-    on_z(6)
+    for p in PIECES:
+        on_y(4, 0, p)
+        on_f(1, p)
+        on_z(5, p)
+        on_z(6, p)
     for d in (1, 3):
         on_x(d, 1, 0)
     ref = b_at(row, 1 - layer, 1 - layer)
     arrived(ref, e_s, e_r)
     to_x(ref, 1, 1)
     to_twin(ref, 3)
-    on_y(2, 0)
+    for p in PIECES:
+        on_y(2, 0, p)
     on_x(2, 0, 0)
     on_x(2, 1, 0)
-    on_y(5, 0)
+    for p in PIECES:
+        on_y(5, 0, p)
     for d in (1, 3, 2):
         on_x(d, 0, 1)
-    on_y(6, 0)
+    for p in PIECES:
+        on_y(6, 0, p)
     for d in (1, 3, 2):
         on_x(d, 1, 1)
-    for n in (3, 4, 2, 5, 6):
-        on_y(n, 1)
-    for n in (0, 3, 4, 2, 5, 6):
-        on_f(n)
-    for m in range(4):
-        on_far(m)
+    for p in PIECES:
+        for n in (0, 3, 4, 2, 5, 6):
+            on_y(n, 1, p)
+            on_f(n, p)
+        for m in range(4):
+            on_far(m, p)
     for n in range(4):
         h, s = (layer, 1 - layer)[n // 2], (layer, 1 - layer)[n % 2]
         arrived(b_at(twin, h, s), t_s.at[n], t_r.at[n])
@@ -232,10 +244,10 @@
         out_specs=(pl.BlockSpec(memory_space=pltpu.VMEM),) * 2,
         scratch_shapes=[
             dma, dma,
-            dma((7,)), dma((7,)),
-            dma((7, 2)), dma((7, 2)),
-            dma((7,)), dma((7,)),
-            dma((4,)), dma((4,)),
+            dma((7, len(PIECES))), dma((7, len(PIECES))),
+            dma((7, 2, len(PIECES))), dma((7, 2, len(PIECES))),
+            dma((7, len(PIECES))), dma((7, len(PIECES))),
+            dma((4, len(PIECES))), dma((4, len(PIECES))),
             dma((4, 3)), dma((4, 3)),
             dma((16,)), dma((16,)),
             dma((2,)),

time: 100 us -> 97.9 us (0.979)
  the two profiles are of different devices: /device:TPU:5 before, /device:TPU:2 now
where the time goes in v5:
time: 97.9 us; the launch traced here: 97 us
  Pallas kernels  92.5 us (94%)
  local copies, waits for them, and re-layouts  3.81 us (4%)
    pallas_call x1, Pallas kernels, gather(): pl.pallas_call(gather_kernel, out_shape=(wide, wide), in_specs=[pl.BlockS...  73.8 us
    pallas_call x1, Pallas kernels, swap(): pl.pallas_call(swap_kernel, out_shape=(out, out), in_specs=[pl.BlockSpec(...  15.4 us
    unnamed x6, local copies, waits for them, and re-layouts  3.81 us
    pallas_call x1, Pallas kernels, multiply(): pl.pallas_call(multiply_kernel, out_shape=jax.ShapeDtypeStruct((HALF, B,...  3.36 us

profile of v5, /device:TPU:2, one launch (start us, length us, event | category | flops | bytes accessed | tf_op | source)
XLA Modules:
  0.0 97.0 jit_solution(9669408776493046939)
XLA Ops:
  0.6 0.0 copy-start
  0.6 1.2 %copy-done = bf16[64,1,1,64,64]{4,3,2,1,0:T(8,128)(2,1)S(1)} copy-done((bf16[64,1,1,64,64]{4,3,2,1,0:T(8,128)(2,1)S(1)}, bf16[64,1,1,64,64]{4,3,2,1,0:T(8,128)(2,1)}, u32[]{:S(2)}) %copy-start) | copy-done | bytes 524312
  1.9 0.0 copy-start.1
  1.9 0.7 copy-done.1
  2.5 73.8 %gather.1 = (bf16[16,2,1040,128]{3,2,1,0:T(8,128)(2,1)S(1)}, bf16[16,2,1040,128]{3,2,1,0:T(8,128)(2,1)S(1)}) custom-call(bf16[64,64,64]{2,1,0:T(8,128)(2,1)S(1)} %bitcast.8, s32[1,64]{1,0:T(1,128)S(1)} %bitcast.11), custom_call_target="tpu_custom_call" | custom-call | tf_op jit(solution)/shard_map/gather/pallas_call | solution.py:240
  76.3 3.4 %multiply.1.acc = f32[32,64,128]{2,1,0:T(8,128)S(1)} custom-call(bf16[16,2,1040,128]{3,2,1,0:T(8,128)(2,1)S(1)} %get-tuple-element.6.a_ref, bf16[16,2,1040,128]{3,2,1,0:T(8,128)(2,1)S(1)} %get-tuple-element.7.b_ref), custom_call_target="tpu_custom_call" | custom-call | tf_op jit(solution)/shard_map/multiply/pallas_call | solution.py:385
  79.7 15.4 %swap.1 = (bf16[64,64,64]{2,1,0:T(8,128)(2,1)S(1)}, bf16[64,64,64]{2,1,0:T(8,128)(2,1)S(1)}) custom-call(f32[32,64,128]{2,1,0:T(8,128)S(1)} %multiply.1.acc, bf16[16,2,1040,128]{3,2,1,0:T(8,128)(2,1)S(1)} %get-tuple-element.6.a_ref), custom_call_target="tpu_custom_call" | custom-call | tf_op jit(solution)/shard_map/swap/pallas_call | solution.py:456
  95.0 1.0 %copy.8 = bf16[64,1,1,64,64]{4,3,2,1,0:T(8,128)(2,1)} copy(bf16[64,1,1,64,64]{4,3,2,1,0:T(8,128)(2,1)S(1)} %bitcast.10) | data formatting | bytes 1048576
  96.0 1.0 copy.9
Async XLA Ops:
  0.6 1.2 %copy-start = (bf16[64,1,1,64,64]{4,3,2,1,0:T(8,128)(2,1)S(1)}, bf16[64,1,1,64,64]{4,3,2,1,0:T(8,128)(2,1)}, u32[]{:S(2)}) copy-start(bf16[64,1,1,64,64]{4,3,2,1,0:T(8,128)(2,1)} %param.2) | copy-start | bytes 1572868
  1.9 0.7 copy-start.1

commit v6 on v5

--- a/solution.py
+++ b/solution.py
@@ -60,7 +60,7 @@
         return jnp.sum(jnp.where(lane == sub + first, number, 0.0), axis=1, keepdims=True)
 
     for h in (0, 1):
-        @pl.loop(0, PAIRS)
+        @pl.loop(0, PAIRS, unroll=4)
         def _(j):
             b_ref[2 * row + h, layer, pl.ds(pl.multiple_of(j * B, B), B), :] = jnp.concatenate(
                 [d_ref[h * HALF + j], d_ref[h * HALF + PAIRS + j]], axis=1
@@ -127,10 +127,10 @@
         send(piece(ref, p), piece(ref, p), g_s.at[m, p], g_r.at[m, p], {"col": at_z(step)})
 
     for p in PIECES:
+        to_z(theirs, theirs, 3, p, other)
+        to_z(theirs, a_at(0, 0), 4, p, aside)
+        to_z(mine, a_at(0, 0), 1, p, {"col": at_z(step)})
         to_y(mine, 0, p)
-        to_z(theirs, theirs, 3, p, other)
-        to_z(mine, a_at(0, 0), 1, p, {"col": at_z(step)})
-        to_z(theirs, a_at(0, 0), 4, p, aside)
         to_z(mine, a_at(0, 0), 2, p, {"col": at_z(4 - step)})
     to_x(mine, 0, 0)
     to_x(theirs, 1, 0)
@@ -399,7 +399,7 @@
     )(a, b)
 
 
-CUTS = 4
+CUTS = 8
 
 
 def swap_kernel(acc, a_ref, sq_ref, ra_ref, out, got, s_sem, r_sem):

time: 97.9 us -> 96.8 us (0.989)
  Pallas kernels: 92.5 us -> 91.5 us
    pallas_call x1, Pallas kernels: 73.8 us -> 72.3 us  [gather(): pl.pallas_call(gather_kernel, out_shape=(wide, wide), in_specs=[pl.BlockS...]
where the time goes in v6:
time: 96.8 us; the launch traced here: 96 us
  Pallas kernels  91.5 us (95%)
  local copies, waits for them, and re-layouts  3.81 us (4%)
    pallas_call x1, Pallas kernels, gather(): pl.pallas_call(gather_kernel, out_shape=(wide, wide), in_specs=[pl.BlockS...  72.3 us
    pallas_call x1, Pallas kernels, swap(): pl.pallas_call(swap_kernel, out_shape=(out, out), in_specs=[pl.BlockSpec(...  15.2 us
    pallas_call x1, Pallas kernels, multiply(): pl.pallas_call(multiply_kernel, out_shape=jax.ShapeDtypeStruct((HALF, B,...  3.97 us
    unnamed x6, local copies, waits for them, and re-layouts  3.81 us

profile of v6, /device:TPU:2, one launch (start us, length us, event | category | flops | bytes accessed | tf_op | source)
XLA Modules:
  0.0 96.0 jit_solution(8079279484107203678)
XLA Ops:
  0.6 0.0 copy-start
  0.6 1.2 %copy-done = bf16[64,1,1,64,64]{4,3,2,1,0:T(8,128)(2,1)S(1)} copy-done((bf16[64,1,1,64,64]{4,3,2,1,0:T(8,128)(2,1)S(1)}, bf16[64,1,1,64,64]{4,3,2,1,0:T(8,128)(2,1)}, u32[]{:S(2)}) %copy-start) | copy-done | bytes 524312
  1.9 0.0 copy-start.1
  1.9 0.7 copy-done.1
  2.5 72.3 %gather.1 = (bf16[16,2,1040,128]{3,2,1,0:T(8,128)(2,1)S(1)}, bf16[16,2,1040,128]{3,2,1,0:T(8,128)(2,1)S(1)}) custom-call(bf16[64,64,64]{2,1,0:T(8,128)(2,1)S(1)} %bitcast.8, s32[1,64]{1,0:T(1,128)S(1)} %bitcast.11), custom_call_target="tpu_custom_call" | custom-call | tf_op jit(solution)/shard_map/gather/pallas_call | solution.py:240
  74.8 4.0 %multiply.1.acc = f32[32,64,128]{2,1,0:T(8,128)S(1)} custom-call(bf16[16,2,1040,128]{3,2,1,0:T(8,128)(2,1)S(1)} %get-tuple-element.6.a_ref, bf16[16,2,1040,128]{3,2,1,0:T(8,128)(2,1)S(1)} %get-tuple-element.7.b_ref), custom_call_target="tpu_custom_call" | custom-call | tf_op jit(solution)/shard_map/multiply/pallas_call | solution.py:385
  78.8 15.2 %swap.1 = (bf16[64,64,64]{2,1,0:T(8,128)(2,1)S(1)}, bf16[64,64,64]{2,1,0:T(8,128)(2,1)S(1)}) custom-call(f32[32,64,128]{2,1,0:T(8,128)S(1)} %multiply.1.acc, bf16[16,2,1040,128]{3,2,1,0:T(8,128)(2,1)S(1)} %get-tuple-element.6.a_ref), custom_call_target="tpu_custom_call" | custom-call | tf_op jit(solution)/shard_map/swap/pallas_call | solution.py:456
  94.0 1.0 %copy.8 = bf16[64,1,1,64,64]{4,3,2,1,0:T(8,128)(2,1)} copy(bf16[64,1,1,64,64]{4,3,2,1,0:T(8,128)(2,1)S(1)} %bitcast.10) | data formatting | bytes 1048576
  95.0 1.0 %copy.9 = bf16[64,1,1,64,64]{4,3,2,1,0:T(8,128)(2,1)} copy(bf16[64,1,1,64,64]{4,3,2,1,0:T(8,128)(2,1)S(1)} %bitcast.9) | data formatting | bytes 1048576
Async XLA Ops:
  0.6 1.2 %copy-start = (bf16[64,1,1,64,64]{4,3,2,1,0:T(8,128)(2,1)S(1)}, bf16[64,1,1,64,64]{4,3,2,1,0:T(8,128)(2,1)}, u32[]{:S(2)}) copy-start(bf16[64,1,1,64,64]{4,3,2,1,0:T(8,128)(2,1)} %param.2) | copy-start | bytes 1572868
  1.9 0.7 copy-start.1

commit v7 on v6

--- a/solution.py
+++ b/solution.py
@@ -25,8 +25,14 @@
     return lax.broadcasted_iota(jnp.int32, (rows, W), 1)
 
 
-def gather_kernel(d_ref, p_ref, a_ref, b_ref,
-                  e_s, e_r, z_s, z_r, y_s, y_r, f_s, f_r, g_s, g_r, x_s, x_r, t_s, t_r, l_s):
+def gather_kernel(d_hbm, p_hbm, a_ref, b_ref, d_ref, p_ref,
+                  e_s, e_r, z_s, z_r, y_s, y_r, f_s, f_r, g_s, g_r, x_s, x_r, t_s, t_r, l_s, i_s):
+    loads = [pltpu.make_async_copy(p_hbm, p_ref, i_s.at[4])]
+    for n in range(4):
+        at = pl.ds(n * PAIRS, PAIRS)
+        loads.append(pltpu.make_async_copy(d_hbm.at[at], d_ref.at[at], i_s.at[n]))
+    for copy in loads:
+        copy.start()
     layer, row, col = lax.axis_index("layer"), lax.axis_index("row"), lax.axis_index("col")
     x, core = row // 2, row % 2
     y, z = col // ZS, col % ZS
@@ -52,6 +58,8 @@
     for peer in peers:
         pl.semaphore_signal(barrier, inc=1, device_id=peer, device_id_type=MESH)
 
+    loads[0].wait()
+
     number = p_ref[...].astype(F32)
     lane = lax.broadcasted_iota(jnp.int32, (PAIRS, B), 1)
     sub = lax.broadcasted_iota(jnp.int32, (PAIRS, B), 0)
@@ -60,6 +68,9 @@
         return jnp.sum(jnp.where(lane == sub + first, number, 0.0), axis=1, keepdims=True)
 
     for h in (0, 1):
+        for copy in loads[1 + 2 * h:3 + 2 * h]:
+            copy.wait()
+
         @pl.loop(0, PAIRS, unroll=4)
         def _(j):
             b_ref[2 * row + h, layer, pl.ds(pl.multiple_of(j * B, B), B), :] = jnp.concatenate(
@@ -240,9 +251,11 @@
     return pl.pallas_call(
         gather_kernel,
         out_shape=(wide, wide),
-        in_specs=[pl.BlockSpec(memory_space=pltpu.VMEM)] * 2,
+        in_specs=[pl.BlockSpec(memory_space=pltpu.HBM)] * 2,
         out_specs=(pl.BlockSpec(memory_space=pltpu.VMEM),) * 2,
         scratch_shapes=[
+            pltpu.VMEM((2 * HALF, B, B), BF16),
+            pltpu.VMEM((1, 2 * HALF), jnp.int32),
             dma, dma,
             dma((7, len(PIECES))), dma((7, len(PIECES))),
             dma((7, 2, len(PIECES))), dma((7, 2, len(PIECES))),
@@ -251,12 +264,13 @@
             dma((4, 3)), dma((4, 3)),
             dma((16,)), dma((16,)),
             dma((2,)),
+            dma((5,)),
         ],
         compiler_params=pltpu.CompilerParams(
             collective_id=0, has_side_effects=True, vmem_limit_bytes=30 << 20
         ),
         name="gather",
-    )(d, p)
+    )(pltpu.with_memory_space_constraint(d, pltpu.HBM), pltpu.with_memory_space_constraint(p, pltpu.HBM))
 
 
 CHUNK = W

time: 96.8 us -> 95.3 us (0.985)
  local copies, waits for them, and re-layouts: 3.81 us -> 1.94 us
    unnamed x6 -> x2, local copies, waits for them, and re-layouts: 3.81 us -> 1.94 us
where the time goes in v7:
time: 95.3 us; the launch traced here: 95 us
  Pallas kernels  92.4 us (97%)
  local copies, waits for them, and re-layouts  1.94 us (2%)
    pallas_call x1, Pallas kernels, gather(): pl.pallas_call(gather_kernel, out_shape=(wide, wide), in_specs=[pl.BlockS...  72.6 us
    pallas_call x1, Pallas kernels, swap(): pl.pallas_call(swap_kernel, out_shape=(out, out), in_specs=[pl.BlockSpec(...  15.8 us
    pallas_call x1, Pallas kernels, multiply(): pl.pallas_call(multiply_kernel, out_shape=jax.ShapeDtypeStruct((HALF, B,...  3.97 us
    unnamed x2, local copies, waits for them, and re-layouts  1.94 us

profile of v7, /device:TPU:2, one launch (start us, length us, event | category | flops | bytes accessed | tf_op | source)
XLA Modules:
  0.0 95.0 jit_solution(15407489503595042169)
XLA Ops:
  0.6 72.6 %gather.1 = (bf16[16,2,1040,128]{3,2,1,0:T(8,128)(2,1)S(1)}, bf16[16,2,1040,128]{3,2,1,0:T(8,128)(2,1)S(1)}) custom-call(bf16[64,64,64]{2,1,0:T(8,128)(2,1)} %bitcast.10, s32[1,64]{1,0:T(1,128)} %bitcast.11), custom_call_target="tpu_custom_call" | custom-call | tf_op jit(solution)/shard_map/gather/pallas_call | solution.py:251
  73.2 4.0 %multiply.1.acc = f32[32,64,128]{2,1,0:T(8,128)S(1)} custom-call(bf16[16,2,1040,128]{3,2,1,0:T(8,128)(2,1)S(1)} %get-tuple-element.6.a_ref, bf16[16,2,1040,128]{3,2,1,0:T(8,128)(2,1)S(1)} %get-tuple-element.7.b_ref), custom_call_target="tpu_custom_call" | custom-call | tf_op jit(solution)/shard_map/multiply/pallas_call | solution.py:399
  77.2 15.8 %swap.1 = (bf16[64,64,64]{2,1,0:T(8,128)(2,1)S(1)}, bf16[64,64,64]{2,1,0:T(8,128)(2,1)S(1)}) custom-call(f32[32,64,128]{2,1,0:T(8,128)S(1)} %multiply.1.acc, bf16[16,2,1040,128]{3,2,1,0:T(8,128)(2,1)S(1)} %get-tuple-element.6.a_ref), custom_call_target="tpu_custom_call" | custom-call | tf_op jit(solution)/shard_map/swap/pallas_call | solution.py:470
  93.0 1.0 %copy.8 = bf16[64,1,1,64,64]{4,3,2,1,0:T(8,128)(2,1)} copy(bf16[64,1,1,64,64]{4,3,2,1,0:T(8,128)(2,1)S(1)} %bitcast.9) | data formatting | bytes 1048576
  94.0 1.0 %copy.9 = bf16[64,1,1,64,64]{4,3,2,1,0:T(8,128)(2,1)} copy(bf16[64,1,1,64,64]{4,3,2,1,0:T(8,128)(2,1)S(1)} %bitcast.8) | data formatting | bytes 1048576

commit v8 on v7

--- a/solution.py
+++ b/solution.py
@@ -485,9 +485,34 @@
     )(acc, a)
 
 
+def store_kernel(sq_ref, ra_ref, sq_out, ra_out, sems):
+    copies = []
+    for n in range(4):
+        at = pl.ds(n * PAIRS, PAIRS)
+        copies.append(pltpu.make_async_copy(sq_ref.at[at], sq_out.at[at], sems.at[0, n]))
+        copies.append(pltpu.make_async_copy(ra_ref.at[at], ra_out.at[at], sems.at[1, n]))
+    for copy in copies:
+        copy.start()
+    for copy in copies:
+        copy.wait()
+
+
+def store(sq, ra):
+    out = jax.ShapeDtypeStruct(sq.shape, BF16)
+    return pl.pallas_call(
+        store_kernel,
+        out_shape=(out, out),
+        in_specs=[pl.BlockSpec(memory_space=pltpu.VMEM)] * 2,
+        out_specs=(pl.BlockSpec(memory_space=pl.ANY),) * 2,
+        scratch_shapes=[pltpu.SemaphoreType.DMA((2, 4))],
+        compiler_params=pltpu.CompilerParams(vmem_limit_bytes=4 << 20),
+        name="store",
+    )(sq, ra)
+
+
 def on_device(density, pattern):
     a, b = gather(density.reshape(2 * HALF, B, B), pattern.reshape(1, 2 * HALF))
-    squared, raised = swap(multiply(a, b), a)
+    squared, raised = store(*swap(multiply(a, b), a))
     return squared.reshape(density.shape), raised.reshape(density.shape)
 
 

time: 95.3 us -> 95.4 us (level)
  the two profiles are of different devices: /device:TPU:2 before, /device:TPU:16 now
where the time goes in v8:
time: 95.4 us; the launch traced here: 95.6 us
  Pallas kernels  95 us (100%)
    pallas_call x1, Pallas kernels, gather(): pl.pallas_call(gather_kernel, out_shape=(wide, wide), in_specs=[pl.BlockS...  70.8 us
    pallas_call x1, Pallas kernels, swap(): pl.pallas_call(swap_kernel, out_shape=(out, out), in_specs=[pl.BlockSpec(...  18.8 us
    pallas_call x1, Pallas kernels, multiply(): pl.pallas_call(multiply_kernel, out_shape=jax.ShapeDtypeStruct((HALF, B,...  3.97 us

profile of v8, /device:TPU:16, one launch (start us, length us, event | category | flops | bytes accessed | tf_op | source)
XLA Modules:
  0.0 95.6 jit_solution(12712463982565769117)
XLA Ops:
  0.6 70.8 %gather.1 = (bf16[16,2,1040,128]{3,2,1,0:T(8,128)(2,1)S(1)}, bf16[16,2,1040,128]{3,2,1,0:T(8,128)(2,1)S(1)}) custom-call(bf16[64,64,64]{2,1,0:T(8,128)(2,1)} %bitcast.8, s32[1,64]{1,0:T(1,128)} %bitcast.9), custom_call_target="tpu_custom_call" | custom-call | tf_op jit(solution)/shard_map/gather/pallas_call | solution.py:251
  71.5 4.0 %multiply.1.acc = f32[32,64,128]{2,1,0:T(8,128)S(1)} custom-call(bf16[16,2,1040,128]{3,2,1,0:T(8,128)(2,1)S(1)} %get-tuple-element.8.a_ref, bf16[16,2,1040,128]{3,2,1,0:T(8,128)(2,1)S(1)} %get-tuple-element.9.b_ref), custom_call_target="tpu_custom_call" | custom-call | tf_op jit(solution)/shard_map/multiply/pallas_call | solution.py:399
  75.4 18.8 %swap.1 = (bf16[64,64,64]{2,1,0:T(8,128)(2,1)S(1)}, bf16[64,64,64]{2,1,0:T(8,128)(2,1)S(1)}) custom-call(f32[32,64,128]{2,1,0:T(8,128)S(1)} %multiply.1.acc, bf16[16,2,1040,128]{3,2,1,0:T(8,128)(2,1)S(1)} %get-tuple-element.8.a_ref), custom_call_target="tpu_custom_call" | custom-call | tf_op jit(solution)/shard_map/swap/pallas_call | solution.py:470
  94.2 1.4 %store.1 = (bf16[64,64,64]{2,1,0:T(8,128)(2,1)}, bf16[64,64,64]{2,1,0:T(8,128)(2,1)}) custom-call(bf16[64,64,64]{2,1,0:T(8,128)(2,1)S(1)} %get-tuple-element.10.sq_ref, bf16[64,64,64]{2,1,0:T(8,128)(2,1)S(1)} %get-tuple-element.11.ra_ref), custom_call_target="tpu_custom_call" | custom-call | tf_op jit(solution)/shard_map/store/pallas_call | solution.py:502
